TPU v7x, 128 devices: a whole 4x4x4 slice. The times are simulated.
128 devices in a mesh: silo: 8 (over z, core), row: 16 (over y, x).
Axes of the slice: x: 4, y: 4, z: 4, core: 2. Of those that a mesh axis runs over, the one named last changes fastest.
Arguments:
- silo_grams: float32 [16, 4096, 4096], P('silo', 'row'), may hold values from -9 to 81, as said below
- silo_weights: bfloat16 [16, 4096, 640], P('silo', 'row'), may hold values from -6 to 6
Outputs:
- merged_rows: float32 [640, 4096], P(('silo', 'row'))
Inputs may be any that keep to these rules, and one draw needn't show every extreme that they name: `silo_grams`: each silo's Gram is symmetric up to float32 rounding and positive definite.
All inputs are finite; a program needn't handle non-finite values.
Results may differ from a plain program's by a relative error of at most 0.0003.
Values may be sent and summed in bfloat16 or wider, within the bound.
A program may use at most 128 MiB of HBM per device.

v0:
```python
import jax
import jax.numpy as jnp
from jax import lax
from jax.sharding import Mesh
from jax.sharding import PartitionSpec as P

ITERS = 2
ROW = ("row_0", "row_1")
SILO_ROW = ("silo", "row_0", "row_1")


full_precision = lax.Precision.HIGHEST


def in_blocks(value, dim, peers):
    lengths = value.shape
    parts = value.reshape(*lengths[:dim], peers, lengths[dim] // peers, *lengths[dim + 1 :])
    return jnp.moveaxis(parts, dim, 0)


def summed_on_arrival(value, axis, dim):
    parts = in_blocks(value, dim, lax.axis_size(axis))
    arrived = lax.all_to_all(parts, axis, split_axis=0, concat_axis=0, tiled=True)
    return arrived.sum(axis=0)


def joined_along(parts, dim):
    lengths = list(parts.shape[1:])
    lengths[dim] *= parts.shape[0]
    return jnp.moveaxis(parts, 0, dim).reshape(lengths)


def sent_to_all(value, axis):
    copies = jnp.broadcast_to(value, (lax.axis_size(axis), *value.shape))
    return lax.all_to_all(copies, axis, split_axis=0, concat_axis=0, tiled=True)


def gathered_copies(value, axis, dim):
    return joined_along(sent_to_all(value, axis), dim)


def one_axis_at_a_time(value, axes):
    for axis in axes:
        value = lax.psum(value, axis)
    return value


def conj_grad(right_side, apply_op, sum_squares, sum_curv):
    solution = jnp.zeros_like(right_side)
    residual = right_side
    direction = right_side
    res_norm = sum_squares(jnp.sum(residual * residual, axis=0))
    for iteration in range(ITERS):
        mapped = apply_op(direction)
        step_size = res_norm / sum_curv(jnp.sum(direction * mapped, axis=0))
        solution = solution + step_size * direction
        residual = residual - step_size * mapped
        if iteration + 1 < ITERS:
            next_norm = sum_squares(jnp.sum(residual * residual, axis=0))
            direction = residual + next_norm / res_norm * direction
            res_norm = next_norm
    return solution


def local(silo_grams, silo_weights):
    partial_op = jnp.sum(silo_grams, axis=0)
    partial_rhs = jnp.einsum(
        "srk,skc->rc",
        silo_grams,
        lax.all_gather(silo_weights, ROW, axis=1, tiled=True).astype(jnp.float32),
        precision=full_precision,
    )
    operator = lax.psum(partial_op, "silo")
    right_side = summed_on_arrival(partial_rhs, "silo", 1)

    def apply_cols(direction):
        return jnp.dot(operator, gathered_copies(direction, ROW, 0), precision=full_precision)

    def squares_cols(values):
        return one_axis_at_a_time(values, ROW)

    def curv_values(values):
        return one_axis_at_a_time(values, ROW)

    solution = conj_grad(right_side, apply_cols, squares_cols, curv_values)
    transposed = solution.T
    return lax.all_to_all(transposed, ROW, split_axis=0, concat_axis=1, tiled=True)


def solution(mesh):
    torus = Mesh(mesh.devices.reshape(mesh.shape["silo"], 4, 4), ("silo", "row_0", "row_1"))
    in_specs = (P("silo", ROW, None), P("silo", ROW, None))
    out_specs = P(SILO_ROW, None)
    return jax.shard_map(local, mesh=torus, in_specs=in_specs, out_specs=out_specs, check_vma=False)
```

profile of v0, /device:TPU:0, one launch (start us, length us, event | category | flops | bytes accessed | tf_op | source)
XLA Modules:
  0.0 250.4 jit_solution(15347304648735894825)
XLA Ops:
  7.4 0.0 all-gather.2.cloned.1.call-start
  7.4 0.7 all-gather.2.cloned.1.call-update
  8.1 0.0 all-reduce.4.cloned.1.call-start
  8.1 6.4 %reduce_sum.56 = f32[256,4096]{1,0:T(8,128)} reduce(f32[2,256,4096]{2,1,0:T(8,128)} %param.2, f32[]{:T(128)} %constant.0.clone.1), dimensions={0}, to_apply=%region_4.0 | reduce | flops 1048576 | bytes 12582916 | tf_op jit(solution)/shard_map/reduce_sum | solution.py:66
  14.6 0.0 all-reduce.4.cloned.1.call-update
  14.6 78.5 %all-gather.2.cloned.1.call-done = bf16[2,4096,640]{2,1,0:T(8,128)(2,1)} async-done(((bf16[2,256,640]{2,1,0:T(8,128)(2,1)}), bf16[2,4096,640]{2,1,0:T(8,128)(2,1)}) %all-gather.2.cloned.1.call-update) | async-done | bytes 10485776 | tf_op jit(solution)/shard_map/all_gather | solution.py:70
  93.1 15.7 %fusion.1 = f32[256,640,1]{0,1,2:T(8,128)S(1)} fusion(f32[2,256,4096]{2,1,0:T(8,128)} %param.2, bf16[2,4096,640]{2,1,0:T(8,128)(2,1)} %all-gather.2.cloned.1.call-done), kind=kOutput, calls=%fused_computation.8 | convolution fusion | flops 16106127360 | bytes 19529728 | tf_op jit(solution)/shard_map/srk,skc->rc/dot_general | solution.py:67
  108.8 16.0 %all_to_all.34 = f32[8,256,80]{1,2,0:T(8,128)S(1)} all-to-all(f32[8,256,80]{1,2,0:T(8,128)S(1)} %bitcast.24), channel_id=1, replica_groups=mesh['silo'=8,'row_0'=4,'row_1'=4] {'silo'}, dimensions={0} | all-to-all | bytes 1310720 | tf_op jit(solution)/shard_map/all_to_all | solution.py:23
  124.9 0.1 broadcast_in_dim.4
  125.0 24.9 %all_to_all.35 = f32[16,256,80]{1,2,0:T(8,128)S(1)} all-to-all(f32[16,256,80]{1,2,0:T(8,128)S(1)} %broadcast_in_dim.4), channel_id=1, replica_groups=mesh['silo'=8,'row_0'=4,'row_1'=4] {'row_0','row_1'}, dimensions={0} | all-to-all | bytes 2621440 | tf_op jit(solution)/shard_map/all_to_all | solution.py:35
  149.9 0.1 copy.14
  150.0 0.0 all-reduce.4.cloned.1.call-done
  150.0 6.2 %multiply_reduce_fusion.1 = (f32[80]{0:T(128)S(1)}, f32[80]{0:T(128)S(1)}, f32[256,80]{0,1:T(8,128)S(1)}) fusion(f32[256,80]{0,1:T(8,128)S(1)} %reduce_sum.54, f32[256,4096]{1,0:T(8,128)} %all-reduce.4.cloned.1.call-done, f32[4096,80]{0,1:T(8,128)S(1)} %bitcast.22), kind=kOutput, calls=%fused_computation.6 | convolution fusion | flops 1006714752 | bytes 5669504 | tf_op jit(solution)/shard_map/dot_general | solution.py:77
  156.3 8.6 %all-reduce.1 = (f32[80]{0:T(128)S(1)}, f32[80]{0:T(128)S(1)}) all-reduce(f32[80]{0:T(128)S(1)} %get-tuple-element.6, f32[80]{0:T(128)S(1)} %get-tuple-element.5), channel_id=1, replica_groups=mesh['silo'=8,'row_0'=4,'row_1'=4] {'row_0'}, use_global_device_ids=true, to_apply=%region_2.0 | all-reduce | flops 160 | bytes 1280 | tf_op jit(solution)/shard_map/psum | solution.py:44
  164.9 8.7 %all-reduce = (f32[80]{0:T(128)S(1)}, f32[80]{0:T(128)S(1)}) all-reduce(f32[80]{0:T(128)S(1)} %get-tuple-element.9, f32[80]{0:T(128)S(1)} %get-tuple-element.10), channel_id=1, replica_groups=mesh['silo'=8,'row_0'=4,'row_1'=4] {'row_1'}, use_global_device_ids=true, to_apply=%region_3.0 | all-reduce | flops 160 | bytes 1280 | tf_op jit(solution)/shard_map/psum | solution.py:44
  173.6 0.2 multiply_reduce_fusion
  173.8 8.6 %psum.68 = f32[80]{0:T(128)S(1)} all-reduce(f32[80]{0:T(128)S(1)} %multiply_reduce_fusion), channel_id=1, replica_groups=mesh['silo'=8,'row_0'=4,'row_1'=4] {'row_0'}, use_global_device_ids=true, to_apply=%region_10.0 | all-reduce | flops 80 | bytes 640 | tf_op jit(solution)/shard_map/psum | solution.py:44
  182.4 9.1 %psum.69 = f32[80]{0:T(128)S(1)} all-reduce(f32[80]{0:T(128)S(1)} %psum.68), channel_id=1, replica_groups=mesh['silo'=8,'row_0'=4,'row_1'=4] {'row_1'}, use_global_device_ids=true, to_apply=%region_11.0 | all-reduce | flops 80 | bytes 640 | tf_op jit(solution)/shard_map/psum | solution.py:44
  191.5 0.0 copy-start
  191.5 0.1 multiply_add_fusion
  191.6 0.1 broadcast_in_dim.5
  191.8 18.1 %all_to_all.36 = f32[16,256,80]{1,2,0:T(8,128)S(1)} all-to-all(f32[16,256,80]{1,2,0:T(8,128)S(1)} %broadcast_in_dim.5), channel_id=1, replica_groups=mesh['silo'=8,'row_0'=4,'row_1'=4] {'row_0','row_1'}, dimensions={0} | all-to-all | bytes 2621440 | tf_op jit(solution)/shard_map/all_to_all | solution.py:35
  209.9 0.1 copy.15
  210.0 0.0 copy-done
  210.0 4.0 %fusion = f32[80]{0:T(128)S(1)} fusion(f32[256,80]{0,1:T(8,128)S(1)} %multiply_add_fusion, f32[256,4096]{1,0:T(8,128)S(1)} %copy-done, f32[4096,80]{0,1:T(8,128)S(1)} %bitcast.23), kind=kOutput, calls=%fused_computation.1 | convolution fusion | flops 1006673856 | bytes 5587264 | tf_op jit(solution)/shard_map/dot_general | solution.py:77
  214.0 8.6 %psum.70 = f32[80]{0:T(128)S(1)} all-reduce(f32[80]{0:T(128)S(1)} %fusion), channel_id=1, replica_groups=mesh['silo'=8,'row_0'=4,'row_1'=4] {'row_0'}, use_global_device_ids=true, to_apply=%region_13.0 | all-reduce | flops 80 | bytes 640 | tf_op jit(solution)/shard_map/psum | solution.py:44
  222.6 8.7 %psum.71 = f32[80]{0:T(128)S(1)} all-reduce(f32[80]{0:T(128)S(1)} %psum.70), channel_id=1, replica_groups=mesh['silo'=8,'row_0'=4,'row_1'=4] {'row_1'}, use_global_device_ids=true, to_apply=%region_14.0 | all-reduce | flops 80 | bytes 640 | tf_op jit(solution)/shard_map/psum | solution.py:44
  231.3 0.1 add_bitcast_fusion
  231.5 10.8 %all_to_all.37 = f32[16,5,256]{2,1,0:T(8,128)S(1)} all-to-all(f32[16,5,256]{2,1,0:T(8,128)S(1)} %all_to_all.26), channel_id=1, replica_groups=mesh['silo'=8,'row_0'=4,'row_1'=4] {'row_0','row_1'}, dimensions={0} | all-to-all | bytes 163840 | tf_op jit(solution)/shard_map/all_to_all | solution.py:87
  242.3 0.7 copy.18
  (5 shorter events, 0.1 us)
Async XLA Ops:
  7.4 85.7 %all-gather.2.cloned.1.call-start = ((), (), s32[]{:S(2)}) async-start(), calls=%async_computation.4 | async-start | bytes 11141120 | tf_op jit(solution)/shard_map/all_gather | solution.py:70
  8.1 141.9 %all-reduce.4.cloned.1.call-start = ((), (), s32[]{:S(2)}) async-start(), calls=%async_computation.5 | async-start | bytes 8388608 | tf_op jit(solution)/shard_map/psum | solution.py:73
  191.5 18.5 %copy-start = (f32[256,4096]{1,0:T(8,128)S(1)}, f32[256,4096]{1,0:T(8,128)}, u32[]{:S(2)}) copy-start(f32[256,4096]{1,0:T(8,128)} %all-reduce.4.cloned.1.call-done) | copy-start | bytes 12582916
Sparse Core Ops, SparseCore 0:
  10.3 82.7 all-gather.1
Sparse Core Ops, SparseCore 1:
  14.7 76.3 all-reduce.3
where the time goes:
time: 251 us; the launch traced here: 250 us
  blocking collectives  122 us (49%)
  waiting for transfers between devices  79.3 us (32%)
  matrix products  26 us (10%)
  between operations  14.9 us (6%)
  other arithmetic  6.85 us (3%)
    all_gather x1, waiting for transfers between devices, local(): lax.all_gather(silo_weights, ROW, axis=1, tiled=True).astype(jnp.float32)  78.5 us
    psum x6, blocking collectives, one_axis_at_a_time(): value = lax.psum(value, axis)  52.3 us
    all_to_all x2, blocking collectives, sent_to_all(): return lax.all_to_all(copies, axis, split_axis=0, concat_axis=0, tiled=True)  43 us
    all_to_all x1, blocking collectives, summed_on_arrival(): lax.all_to_all(parts, axis, split_axis=0, concat_axis=0, tiled=True)  16 us
    dot_general x1, matrix products, local(): jnp.einsum('srk,skc->rc', silo_grams, lax.all_gather(silo_weights, ROW, a...  15.7 us
    all_to_all x1, blocking collectives, local(): lax.all_to_all(transposed, ROW, split_axis=0, concat_axis=1, tiled=True)  10.8 us
    dot_general x2, matrix products, apply_cols(): jnp.dot(operator, gathered_copies(direction, ROW, 0), precision=full_prec...  10.3 us
    reduce_sum x1, other arithmetic, local(): partial_op = jnp.sum(silo_grams, axis=0)  6.42 us
  transfers between devices with their start and end apart: 2, of which 1 were waited for; matrix products, arithmetic and copies ran while one was open for 9% of the time, Pallas kernels for 0%

commit v1 on v0

v1 whole, which is shorter than its diff:
```python
import jax
import jax.numpy as jnp
from jax import lax
from jax.experimental import pallas as pl
from jax.experimental.pallas import tpu as pltpu
from jax.sharding import Mesh
from jax.sharding import PartitionSpec as P

F32, BF16 = jnp.float32, jnp.bfloat16
MESH = pl.DeviceIdType.MESH
AXES = ("z", "core", "y", "x")
NT = (((1,), (1,)), ((), ()))
NN = (((1,), (0,)), ((), ()))
NEAR = (1, 3, 2)


def dot(a, b, dims=NN, precision=None):
    return lax.dot_general(a, b, dims, precision=precision, preferred_element_type=F32)


def halves(value):
    high = value.astype(BF16)
    return high, (value - high.astype(F32)).astype(BF16)


def kernel(
    g_hbm, w_ref, out_ref,
    g, gh, gl, wt, p, q, r, far, near, second, third,
    ap, a_sib, a_rs, a_op, bg, qg, pg, tiny,
    load_sem, s_sib, r_sib, s_one, r_one, s_two, r_two, s_z, r_z,
    s_asib, r_asib, s_ars, r_ars, s_aag, r_aag, s_afw, r_afw,
    s_b, r_b, s_q, r_q, s_t, r_t,
):
    z, k, y, x = (lax.axis_index(a) for a in AXES)

    def dxy(i, j):
        return (1 - k) * i + k * j, (1 - k) * j + k * i

    def block_row(i, j):
        dx, dy = dxy(i, j)
        return lax.rem(y + dy, 4) * 4 + lax.rem(x + dx, 4)

    def canon(i, j):
        dx, dy = dxy(i, j)
        return dx * 4 + dy

    def plane_peer(i, j):
        dx, dy = dxy(i, j)
        return (z, k, lax.rem(y + dy, 4), lax.rem(x + dx, 4))

    def z_peer(d):
        return (lax.rem(z + d, 4), k, y, x)

    sibling = (z, 1 - k, y, x)

    def remote(src, dst, ssem, rsem, device):
        return pltpu.make_async_remote_copy(src, dst, ssem, rsem, device_id=device, device_id_type=MESH)

    sent = []

    def send(*args):
        copy = remote(*args)
        copy.start()
        sent.append(copy)

    def arrived(dst, ssem, rsem):
        remote(dst, dst, ssem, rsem, sibling).wait_recv()

    barrier = pltpu.get_barrier_semaphore()
    others = [(i, j) for i in range(4) for j in range(4) if i or j]
    for i, j in others:
        pl.semaphore_signal(barrier, 1, device_id=plane_peer(i, j), device_id_type=MESH)
    for d in NEAR:
        pl.semaphore_signal(barrier, 1, device_id=z_peer(d), device_id_type=MESH)
    pl.semaphore_signal(barrier, 1, device_id=sibling, device_id_type=MESH)

    def load(i, j):
        col = pl.multiple_of(block_row(i, j) * 256, 256)
        return pltpu.make_async_copy(g_hbm.at[:, :, pl.ds(col, 256)], g.at[4 * i + j], load_sem.at[4 * i + j])

    order = [(i, 2) for i in range(4)] + [(2, j) for j in (0, 1, 3)]
    order += [(i, j) for j in (1, 3) for i in (0, 1, 3)] + [(1, 0), (3, 0), (0, 0)]
    for i, j in order:
        load(i, j).start()

    flipped = w_ref[...].reshape(512, 640).astype(F32).T.astype(BF16)
    for s in range(8):
        wt[s % 2, s // 2] = flipped[s * 80 : (s + 1) * 80]

    def split(i, j):
        load(i, j).wait()
        value = g[4 * i + j]
        high, low = halves(value)
        gh[4 * i + j] = high.reshape(512, 256)
        gl[4 * i + j] = low.reshape(512, 256)
        ap[canon(i, j)] = value[0] + value[1]

    def tile(core, slot):
        w = wt[core].reshape(320, 512)
        return (dot(w, gh[slot]) + dot(w, gl[slot])).reshape(4, 80, 256)

    def for_sibling(m):
        def body(n, carry):
            q[4 * m + n] = tile(1 - k, 4 * n + m)
            return carry

        lax.fori_loop(0, 4, body, 0)
        rows = pl.ds(4 * m, 4)
        send(q.at[rows], r.at[rows], s_sib.at[m], r_sib.at[m], sibling)

    def for_self(m):
        def body(n, carry):
            p[4 * m + n] = tile(k, 4 * m + n)
            return carry

        lax.fori_loop(0, 4, body, 0)

    def add_sibling(m):
        rows = pl.ds(4 * m, 4)
        arrived(r.at[rows], s_sib.at[m], r_sib.at[m])

        def body(n, carry):
            p[4 * m + n] += r[4 * m + n]
            return carry

        lax.fori_loop(0, 4, body, 0)

    up, down = plane_peer(1, 0), plane_peer(3, 0)

    for i in range(4):
        split(i, 2)
    pl.semaphore_wait(barrier, 19)
    for_sibling(2)
    for j in (0, 1, 3):
        split(2, j)
    for_self(2)
    add_sibling(2)
    send(p.at[pl.ds(8, 2)], far.at[0], s_one.at[0], r_one.at[0], up)
    send(p.at[pl.ds(10, 2)], far.at[1], s_one.at[1], r_one.at[1], down)
    for j in (1, 3):
        for i in (0, 1, 3):
            split(i, j)
        for_sibling(j)
    for i in (1, 3):
        split(i, 0)
    for_self(1)
    add_sibling(1)
    send(p.at[pl.ds(6, 2)], near.at[0, 1], s_one.at[2], r_one.at[2], up)
    for_self(3)
    add_sibling(3)
    send(p.at[pl.ds(12, 2)], near.at[1, 0], s_one.at[3], r_one.at[3], down)
    split(0, 0)

    mine, theirs = pl.ds(8 * k, 8), pl.ds(8 * (1 - k), 8)
    send(ap.at[theirs], a_sib, s_asib.at[0], r_asib.at[0], sibling)
    for_sibling(0)
    for_self(0)
    arrived(a_sib, s_asib.at[0], r_asib.at[0])

    def add_op(n, carry):
        a_sib[n] += ap[8 * k + n]
        return carry

    lax.fori_loop(0, 8, add_op, 0)
    for d in NEAR:
        at = pl.ds(2 * lax.rem(z + d, 4), 2)
        send(a_sib.at[at], a_rs.at[3 - d], s_ars.at[3 - d], r_ars.at[3 - d], z_peer(d))
    add_sibling(0)

    arrived(far.at[0], s_one.at[0], r_one.at[0])
    for n in range(2):
        p[4 + n] += far[0, n]
    send(p.at[pl.ds(4, 2)], near.at[0, 0], s_one.at[4], r_one.at[4], up)
    arrived(far.at[1], s_one.at[1], r_one.at[1])
    for n in range(2):
        p[14 + n] += far[1, n]
    send(p.at[pl.ds(14, 2)], near.at[1, 1], s_one.at[5], r_one.at[5], down)

    for d in NEAR:
        arrived(a_rs.at[3 - d], s_ars.at[3 - d], r_ars.at[3 - d])
    own = 8 * k + 2 * z
    for n in range(2):
        total = a_sib[2 * z + n] + a_rs[0, n] + a_rs[1, n] + a_rs[2, n]
        high, low = halves(total)
        a_op[own + n, 0] = high
        a_op[own + n, 1] = low
    for d in NEAR:
        at = pl.ds(own, 2)
        send(a_op.at[at], a_op.at[at], s_aag.at[3 - d], r_aag.at[3 - d], z_peer(d))
    send(a_op.at[pl.ds(own, 2)], a_op.at[pl.ds(own, 2)], s_afw.at[0], r_afw.at[0], sibling)

    arrived(near.at[0, 1], s_one.at[2], r_one.at[2])
    arrived(near.at[1, 0], s_one.at[3], r_one.at[3])
    arrived(near.at[0, 0], s_one.at[4], r_one.at[4])
    arrived(near.at[1, 1], s_one.at[5], r_one.at[5])
    for h in (1, 0):
        for n in range(2):
            p[2 * h + n] += near[0, h, n] + near[1, h, n]

    for d in NEAR:
        send(p.at[d], second.at[3 - d], s_two.at[3 - d], r_two.at[3 - d], plane_peer(0, d))
    for d in NEAR:
        arrived(second.at[3 - d], s_two.at[3 - d], r_two.at[3 - d])
    p[0] += second[0] + second[1] + second[2]

    for d in NEAR:
        send(p.at[0, lax.rem(z + d, 4)], third.at[3 - d], s_z.at[3 - d], r_z.at[3 - d], z_peer(d))
    for d in NEAR:
        arrived(third.at[3 - d], s_z.at[3 - d], r_z.at[3 - d])
    right = p[0, z] + third[0] + third[1] + third[2]

    def gather(buf, value, ss, rs, use):
        high, low = halves(value)
        buf[0, 0:80] = high
        buf[0, 80:160] = low
        for d in NEAR:
            send(buf.at[0], buf.at[16 - 4 * d], ss.at[16 - 4 * d], rs.at[16 - 4 * d], plane_peer(d, 0))
            send(buf.at[0], buf.at[4 - d], ss.at[4 - d], rs.at[4 - d], plane_peer(0, d))
        use(0, 0)
        for i in NEAR:
            arrived(buf.at[4 * i], ss.at[4 * i], rs.at[4 * i])
            for d in NEAR:
                at = 4 * i + 4 - d
                send(buf.at[4 * i], buf.at[at], ss.at[at], rs.at[at], plane_peer(0, d))
        for i in NEAR:
            use(i, 0)
        for i in (0, 1, 3, 2):
            for j in NEAR:
                at = 4 * i + j
                arrived(buf.at[at], ss.at[at], rs.at[at])
                use(i, j)

    def whole(buf, slot):
        return buf[slot, 0:80].astype(F32) + buf[slot, 80:160].astype(F32)

    def apply_op(buf):
        def body(n, total):
            i, j = n // 4, n % 4
            at = canon(i, j)
            wide = dot(buf[n], a_op[at, 0], NT)
            return total + wide[0:80] + wide[80:160] + dot(buf[n, 0:80], a_op[at, 1], NT)

        return lax.fori_loop(0, 16, body, jnp.zeros((80, 256), F32))

    gather(bg, right, s_b, r_b, lambda i, j: None)

    for d in NEAR:
        at = pl.ds(8 * k + 2 * lax.rem(z + d, 4), 2)
        arrived(a_op.at[at], s_aag.at[d - 1], r_aag.at[d - 1])
        send(a_op.at[at], a_op.at[at], s_afw.at[d], r_afw.at[d], sibling)
    for d in range(4):
        at = pl.ds(8 * (1 - k) + 2 * lax.rem(z + d, 4), 2)
        arrived(a_op.at[at], s_afw.at[d], r_afw.at[d])

    mapped = apply_op(bg)
    gather(qg, mapped, s_q, r_q, lambda i, j: None)

    zero = jnp.zeros((80, 256), F32)

    def sums(n, carry):
        b, m = whole(bg, n), whole(qg, n)
        return carry[0] + b * b, carry[1] + b * m

    norm, curv = lax.fori_loop(0, 16, sums, (zero, zero))
    norm = jnp.sum(norm, axis=1, keepdims=True)
    step = norm / jnp.sum(curv, axis=1, keepdims=True)

    def residuals(n, total):
        res = whole(bg, n) - step * whole(qg, n)
        return total + res * res

    beta = jnp.sum(lax.fori_loop(0, 16, residuals, zero), axis=1, keepdims=True) / norm

    def directions(n, carry):
        b = whole(bg, n)
        high, low = halves(b - step * whole(qg, n) + beta * b)
        pg[n, 0:80] = high
        pg[n, 80:160] = low
        return carry

    lax.fori_loop(0, 16, directions, 0)
    product = whole(pg, 0) * apply_op(pg)
    product = jnp.concatenate([product, jnp.zeros((48, 256), F32)], axis=0)
    tiny[0] = dot(jnp.ones((8, 256), F32), product, NT, lax.Precision.HIGHEST)
    for i, j in others:
        at = (4 - i) % 4 * 4 + (4 - j) % 4
        send(tiny.at[0], tiny.at[at], s_t.at[at], r_t.at[at], plane_peer(i, j))

    first = 5 * (4 * y + x)
    line = lax.broadcasted_iota(jnp.int32, (16, 80), 0)
    column = lax.broadcasted_iota(jnp.int32, (16, 80), 1)
    pick = jnp.where((line < 5) & (column == line + first), 1.0, 0.0).astype(BF16)

    def picked(buf, n):
        return (dot(pick, buf[n, 0:80]) + dot(pick, buf[n, 80:160]))[0:8]

    bs = [picked(bg, n) for n in range(16)]
    ms = [picked(qg, n) for n in range(16)]

    def row_sum(parts):
        total = parts[0]
        for part in parts[1:]:
            total = total + part
        return jnp.sum(total, axis=1, keepdims=True)

    norm5 = row_sum([b * b for b in bs])
    step5 = norm5 / row_sum([b * m for b, m in zip(bs, ms)])
    rs = [b - step5 * m for b, m in zip(bs, ms)]
    next5 = row_sum([v * v for v in rs])
    ps = [v + next5 / norm5 * b for v, b in zip(rs, bs)]

    for i, j in others:
        at = 4 * i + j
        arrived(tiny.at[at], s_t.at[at], r_t.at[at])
    curv = tiny[0]
    for n in range(1, 16):
        curv = curv + tiny[n]
    line = lax.broadcasted_iota(jnp.int32, (8, 128), 0)
    column = lax.broadcasted_iota(jnp.int32, (8, 128), 1)
    curv = jnp.sum(jnp.where(column == line + first, curv, 0.0), axis=1, keepdims=True)
    step2 = next5 / curv
    for i in range(4):
        for j in range(4):
            n = 4 * i + j
            value = step5 * bs[n] + step2 * ps[n]
            col = pl.multiple_of(block_row(i, j) * 256, 256)
            out_ref[:, pl.ds(col, 256)] = value[0:5]
    for copy in sent:
        copy.wait_send()


def local(silo_grams, silo_weights):
    dma = pltpu.SemaphoreType.DMA
    scratch = [
        pltpu.VMEM((16, 2, 256, 256), F32),
        pltpu.VMEM((16, 512, 256), BF16),
        pltpu.VMEM((16, 512, 256), BF16),
        pltpu.VMEM((2, 4, 80, 512), BF16),
        pltpu.VMEM((16, 4, 80, 256), F32),
        pltpu.VMEM((16, 4, 80, 256), F32),
        pltpu.VMEM((16, 4, 80, 256), F32),
        pltpu.VMEM((2, 2, 4, 80, 256), F32),
        pltpu.VMEM((2, 2, 2, 4, 80, 256), F32),
        pltpu.VMEM((3, 4, 80, 256), F32),
        pltpu.VMEM((3, 80, 256), F32),
        pltpu.VMEM((16, 256, 256), F32),
        pltpu.VMEM((8, 256, 256), F32),
        pltpu.VMEM((3, 2, 256, 256), F32),
        pltpu.VMEM((16, 2, 256, 256), BF16),
        pltpu.VMEM((16, 160, 256), BF16),
        pltpu.VMEM((16, 160, 256), BF16),
        pltpu.VMEM((16, 160, 256), BF16),
        pltpu.VMEM((16, 8, 128), F32),
    ]
    counts = [16, 4, 4, 6, 6, 3, 3, 3, 3, 1, 1, 3, 3, 3, 3, 4, 4, 16, 16, 16, 16, 16, 16]
    scratch += [dma((n,)) for n in counts]
    return pl.pallas_call(
        kernel,
        out_shape=jax.ShapeDtypeStruct((5, 4096), F32),
        in_specs=[pl.BlockSpec(memory_space=pl.ANY), pl.BlockSpec(memory_space=pltpu.VMEM)],
        out_specs=pl.BlockSpec(memory_space=pltpu.VMEM),
        scratch_shapes=scratch,
        compiler_params=pltpu.CompilerParams(collective_id=0, has_side_effects=True, vmem_limit_bytes=62 << 20),
        cost_estimate=pl.CostEstimate(flops=6_500_000_000, bytes_accessed=9_200_000, transcendentals=0),
    )(silo_grams, silo_weights)


def solution(mesh):
    torus = Mesh(mesh.devices.reshape(4, 2, 4, 4), AXES)
    silo, row = ("z", "core"), ("y", "x")
    in_specs = (P(silo, row, None), P(silo, row, None))
    out_specs = P(silo + row, None)
    return jax.shard_map(local, mesh=torus, in_specs=in_specs, out_specs=out_specs, check_vma=False)
```

time: 251 us -> 125 us (0.50)
  the two profiles are of different devices: /device:TPU:0 before, /device:TPU:1 now
where the time goes in v1:
time: 125 us
  Pallas kernels  123 us (98%)
  local copies, waits for them, and re-layouts  1.57 us (1%)
    pallas_call x1, Pallas kernels, local(): pl.pallas_call(kernel, out_shape=jax.ShapeDtypeStruct((5, 4096), F32), in...  123 us

profile of v1, /device:TPU:1, one launch (start us, length us, event | category | flops | bytes accessed | tf_op | source)
XLA Modules:
  0.0 125.0 jit_solution(16100533184821821872)
XLA Ops:
  0.0 123.5 %shard_map.28 = f32[5,4096]{1,0:T(8,128)} custom-call(f32[2,256,4096]{2,1,0:T(8,128)} %g_hbm.1, bf16[2,256,640]{2,1,0:T(8,128)(2,1)} %w_ref.1), custom_call_target="tpu_custom_call" | custom-call | flops 6499999744 | bytes 9200000 | tf_op jit(solution)/shard_map/pallas_call | solution.py:357
  123.5 1.6 %copy.4 = f32[5,4096]{1,0:T(8,128)} copy(f32[5,4096]{1,0:T(8,128)} %shard_map.28) | data formatting | bytes 163840

commit v2 on v1

v2 whole, which is shorter than its diff:
```python
import jax
import jax.numpy as jnp
from jax import lax
from jax.experimental import pallas as pl
from jax.experimental.pallas import tpu as pltpu
from jax.sharding import Mesh
from jax.sharding import PartitionSpec as P

F32, BF16 = jnp.float32, jnp.bfloat16
MESH = pl.DeviceIdType.MESH
AXES = ("z", "core", "y", "x")
NT = (((1,), (1,)), ((), ()))
NN = (((1,), (0,)), ((), ()))
NEAR = (1, 3, 2)
FAR = (2, 1, 3, 0)


def dot(a, b, dims=NN, precision=None):
    return lax.dot_general(a, b, dims, precision=precision, preferred_element_type=F32)


def halves(value):
    high = value.astype(BF16)
    return high, (value - high.astype(F32)).astype(BF16)


def kernel(
    g_hbm, w_hbm, out_ref,
    w_raw, g, gh, gl, wt, p, q, r, far, near, second, third,
    ap, a_sib, a_far, a_near, a_op, bg, qg, pg, tiny,
    w_sem, load_sem, s_sib, r_sib, s_one, r_one, s_two, r_two, s_z, r_z,
    s_asib, r_asib, s_ars, r_ars, s_aag, r_aag, s_afw, r_afw,
    s_b, r_b, s_q, r_q, s_t, r_t,
):
    z, k, y, x = (lax.axis_index(a) for a in AXES)

    def dxy(i, j):
        return (1 - k) * i + k * j, (1 - k) * j + k * i

    def block_row(i, j):
        dx, dy = dxy(i, j)
        return lax.rem(y + dy, 4) * 4 + lax.rem(x + dx, 4)

    def canon(i, j):
        dx, dy = dxy(i, j)
        return dx * 4 + dy

    def plane_peer(i, j):
        dx, dy = dxy(i, j)
        return (z, k, lax.rem(y + dy, 4), lax.rem(x + dx, 4))

    def z_peer(d):
        return (lax.rem(z + d, 4), k, y, x)

    sibling = (z, 1 - k, y, x)

    def remote(src, dst, ssem, rsem, device):
        return pltpu.make_async_remote_copy(src, dst, ssem, rsem, device_id=device, device_id_type=MESH)

    sent = []

    def send(*args):
        copy = remote(*args)
        copy.start()
        sent.append(copy)

    def arrived(dst, rsem):
        remote(dst, dst, s_sib.at[0], rsem, sibling).wait_recv()

    weights = pltpu.make_async_copy(w_hbm, w_raw, w_sem.at[0])
    weights.start()

    def load(i, j):
        col = pl.multiple_of(block_row(i, j) * 256, 256)
        return pltpu.make_async_copy(g_hbm.at[:, :, pl.ds(col, 256)], g.at[4 * i + j], load_sem.at[4 * i + j])

    early = [(i, 2) for i in range(4)] + [(2, j) for j in (0, 1, 3)]
    late = [(i, j) for j in (1, 3) for i in (0, 1, 3)] + [(1, 0), (3, 0), (0, 0)]
    for i, j in early + late:
        load(i, j).start()

    barrier = pltpu.get_barrier_semaphore()
    others = [(i, j) for i in FAR for j in FAR if i or j]
    for i, j in others:
        pl.semaphore_signal(barrier, 1, device_id=plane_peer(i, j), device_id_type=MESH)
    for d in NEAR:
        pl.semaphore_signal(barrier, 1, device_id=z_peer(d), device_id_type=MESH)
    pl.semaphore_signal(barrier, 1, device_id=sibling, device_id_type=MESH)

    weights.wait()
    flipped = w_raw[...].reshape(512, 640).astype(F32).T.astype(BF16)
    for s in range(8):
        wt[s % 2, lax.rem(s // 2 + 4 - z, 4)] = flipped[s * 80 : (s + 1) * 80]

    def split(i, j):
        load(i, j).wait()
        value = g[4 * i + j]
        high, low = halves(value)
        gh[4 * i + j] = high.reshape(512, 256)
        gl[4 * i + j] = low.reshape(512, 256)
        ap[canon(i, j)] = value[0] + value[1]

    def tile(core, slot):
        w = wt[core].reshape(320, 512)
        return (dot(w, gh[slot]) + dot(w, gl[slot])).reshape(4, 80, 256)

    def loop(count, step):
        def body(n, carry):
            step(n)
            return carry

        lax.fori_loop(0, count, body, 0)

    def for_sibling(m, lo, count, sem):
        def step(n):
            q[4 * m + lo + n] = tile(1 - k, 4 * (lo + n) + m)

        loop(count, step)
        rows = pl.ds(4 * m + lo, count)
        send(q.at[rows], r.at[rows], s_sib.at[sem], r_sib.at[sem], sibling)

    def for_self(m, lo, count):
        def step(n):
            p[4 * m + lo + n] = tile(k, 4 * m + lo + n)

        loop(count, step)

    def add_sibling(m, lo, count, sem):
        rows = pl.ds(4 * m + lo, count)
        arrived(r.at[rows], r_sib.at[sem])

        def step(n):
            p[4 * m + lo + n] += r[4 * m + lo + n]

        loop(count, step)

    up, down = plane_peer(1, 0), plane_peer(3, 0)

    split(0, 2)
    split(1, 2)
    pl.semaphore_wait(barrier, 19)
    for_sibling(2, 0, 2, 0)
    split(2, 2)
    split(3, 2)
    for_sibling(2, 2, 2, 1)
    split(2, 0)
    split(2, 1)
    for_self(2, 0, 2)
    add_sibling(2, 0, 2, 0)
    send(p.at[pl.ds(8, 2)], far.at[0], s_one.at[0], r_one.at[0], up)
    split(2, 3)
    for_self(2, 2, 2)
    add_sibling(2, 2, 2, 1)
    send(p.at[pl.ds(10, 2)], far.at[1], s_one.at[1], r_one.at[1], down)

    for i, j in late:
        split(i, j)
    mine, theirs = pl.ds(8 * k, 8), pl.ds(8 * (1 - k), 8)
    send(ap.at[theirs], a_sib, s_asib.at[0], r_asib.at[0], sibling)

    for_sibling(1, 0, 4, 2)
    for_self(1, 0, 4)
    for_sibling(3, 0, 4, 3)
    add_sibling(1, 0, 4, 2)
    send(p.at[pl.ds(6, 2)], near.at[0, pl.ds(2, 2)], s_one.at[2], r_one.at[2], up)
    for_self(3, 0, 4)
    add_sibling(3, 0, 4, 3)
    send(p.at[pl.ds(12, 2)], near.at[1, pl.ds(0, 2)], s_one.at[3], r_one.at[3], down)

    arrived(a_sib, r_asib.at[0])

    def add_op(n):
        a_sib[n] += ap[8 * k + n]

    loop(8, add_op)

    def quarter(d, n):
        return 2 * lax.rem(z + d, 4) + n

    z_up, z_down = z_peer(1), z_peer(3)
    send(a_sib.at[quarter(2, 0)], a_far.at[0], s_ars.at[0], r_ars.at[0], z_up)
    send(a_sib.at[quarter(2, 1)], a_far.at[1], s_ars.at[1], r_ars.at[1], z_down)
    send(a_sib.at[quarter(1, 1)], a_near.at[0, 1], s_ars.at[2], r_ars.at[2], z_up)
    send(a_sib.at[quarter(3, 0)], a_near.at[1, 0], s_ars.at[3], r_ars.at[3], z_down)
    for_sibling(0, 0, 4, 4)
    for_self(0, 0, 4)
    add_sibling(0, 0, 4, 4)

    arrived(far.at[0], r_one.at[0])
    for n in (1, 0):
        p[4 + n] += far[0, n]
        send(p.at[4 + n], near.at[0, n], s_one.at[4 + n], r_one.at[4 + n], up)
    arrived(far.at[1], r_one.at[1])
    for n in range(2):
        p[14 + n] += far[1, n]
        send(p.at[14 + n], near.at[1, 2 + n], s_one.at[6 + n], r_one.at[6 + n], down)

    arrived(a_far.at[0], r_ars.at[0])
    a_sib[quarter(1, 0)] += a_far[0]
    send(a_sib.at[quarter(1, 0)], a_near.at[0, 0], s_ars.at[4], r_ars.at[4], z_up)
    arrived(a_far.at[1], r_ars.at[1])
    a_sib[quarter(3, 1)] += a_far[1]
    send(a_sib.at[quarter(3, 1)], a_near.at[1, 1], s_ars.at[5], r_ars.at[5], z_down)

    def second_axis(d):
        send(p.at[d, pl.ds(1, 3)], second.at[3 - d, pl.ds(1, 3)], s_two.at[3 - d], r_two.at[3 - d], plane_peer(0, d))
        send(p.at[d, 0], second.at[3 - d, 0], s_two.at[6 - d], r_two.at[6 - d], plane_peer(0, d))

    def whole_sum(n):
        p[n] += near[0, n] + near[1, n]

    arrived(near.at[0, pl.ds(2, 2)], r_one.at[2])
    arrived(near.at[1, pl.ds(0, 2)], r_one.at[3])
    arrived(near.at[0, 1], r_one.at[5])
    whole_sum(1)
    second_axis(1)
    arrived(near.at[1, 2], r_one.at[6])
    whole_sum(2)
    second_axis(2)
    arrived(near.at[1, 3], r_one.at[7])
    whole_sum(3)
    second_axis(3)
    arrived(near.at[0, 0], r_one.at[4])
    whole_sum(0)

    arrived(a_near.at[0, 1], r_ars.at[2])
    arrived(a_near.at[1, 0], r_ars.at[3])
    arrived(a_near.at[0, 0], r_ars.at[4])
    arrived(a_near.at[1, 1], r_ars.at[5])

    def op_rows(d):
        return pl.ds(8 * k + quarter(d, 0), 2)

    own = 8 * k + quarter(0, 0)
    for n in range(2):
        high, low = halves(a_sib[quarter(0, n)] + a_near[0, n] + a_near[1, n])
        a_op[own + n, 0] = high
        a_op[own + n, 1] = low
    send(a_op.at[op_rows(0)], a_op.at[op_rows(0)], s_aag.at[0], r_aag.at[0], z_up)
    send(a_op.at[op_rows(0)], a_op.at[op_rows(0)], s_aag.at[1], r_aag.at[1], z_down)
    send(a_op.at[op_rows(0)], a_op.at[op_rows(0)], s_afw.at[0], r_afw.at[0], sibling)

    for d in NEAR:
        arrived(second.at[3 - d, pl.ds(1, 3)], r_two.at[3 - d])
    for d in NEAR:
        p[0, d] += second[0, d] + second[1, d] + second[2, d]
        send(p.at[0, d], third.at[3 - d], s_z.at[3 - d], r_z.at[3 - d], z_peer(d))
    for d in NEAR:
        arrived(second.at[3 - d, 0], r_two.at[6 - d])
    right = p[0, 0] + second[0, 0] + second[1, 0] + second[2, 0]

    arrived(a_op.at[op_rows(3)], r_aag.at[0])
    at = 8 * k + quarter(3, 0)
    send(a_op.at[at], a_op.at[at], s_aag.at[2], r_aag.at[2], z_up)
    send(a_op.at[op_rows(3)], a_op.at[op_rows(3)], s_afw.at[1], r_afw.at[1], sibling)
    arrived(a_op.at[op_rows(1)], r_aag.at[1])
    at = 8 * k + quarter(1, 1)
    send(a_op.at[at], a_op.at[at], s_aag.at[3], r_aag.at[3], z_down)
    send(a_op.at[op_rows(1)], a_op.at[op_rows(1)], s_afw.at[2], r_afw.at[2], sibling)

    for d in NEAR:
        arrived(third.at[3 - d], r_z.at[3 - d])
    right = right + third[0] + third[1] + third[2]

    def spread(buf, value, ss, rs):
        high, low = halves(value)
        buf[0, 0:80] = high
        buf[0, 80:160] = low
        for d in NEAR:
            send(buf.at[0], buf.at[16 - 4 * d], ss.at[16 - 4 * d], rs.at[16 - 4 * d], plane_peer(d, 0))
        for d in NEAR:
            send(buf.at[0], buf.at[4 - d], ss.at[4 - d], rs.at[4 - d], plane_peer(0, d))

    def pass_on(buf, ss, rs):
        for i in NEAR:
            arrived(buf.at[4 * i], rs.at[4 * i])
            for d in NEAR:
                at = 4 * i + 4 - d
                send(buf.at[4 * i], buf.at[at], ss.at[at], rs.at[at], plane_peer(0, d))

    def collect(buf, rs, use):
        for i in range(4):
            use(4 * i)
        for i in (0, 1, 3, 2):
            for j in NEAR:
                at = 4 * i + j
                arrived(buf.at[at], rs.at[at])
                use(at)

    def whole(buf, slot):
        return buf[slot, 0:80].astype(F32) + buf[slot, 80:160].astype(F32)

    def op_term(buf, n):
        at = canon(n // 4, n % 4)
        wide = dot(buf[n], a_op[at, 0], NT)
        return wide[0:80] + wide[80:160] + dot(buf[n, 0:80], a_op[at, 1], NT)

    zero = jnp.zeros((80, 256), F32)
    spread(bg, right, s_b, r_b)
    pass_on(bg, s_b, r_b)

    for n in range(2):
        at = 8 * k + quarter(2, n)
        arrived(a_op.at[at], r_aag.at[2 + n])
        send(a_op.at[at], a_op.at[at], s_afw.at[3 + n], r_afw.at[3 + n], sibling)
    theirs = 8 * (1 - k)
    for n, d in enumerate((0, 3, 1)):
        arrived(a_op.at[pl.ds(theirs + quarter(d, 0), 2)], r_afw.at[n])
    for n in range(2):
        arrived(a_op.at[theirs + quarter(2, n)], r_afw.at[3 + n])

    total = [zero, zero]

    def use_right(n):
        total[0] = total[0] + op_term(bg, n)
        b = whole(bg, n)
        total[1] = total[1] + b * b

    collect(bg, r_b, use_right)
    mapped, norm = total
    norm = jnp.sum(norm, axis=1, keepdims=True)
    spread(qg, mapped, s_q, r_q)
    pass_on(qg, s_q, r_q)
    total = [zero]

    def use_mapped(n):
        total[0] = total[0] + whole(bg, n) * whole(qg, n)

    collect(qg, r_q, use_mapped)
    step = norm / jnp.sum(total[0], axis=1, keepdims=True)

    def residuals(n, total):
        res = whole(bg, n) - step * whole(qg, n)
        return total + res * res

    beta = jnp.sum(lax.fori_loop(0, 16, residuals, zero), axis=1, keepdims=True) / norm

    def directions(n, total):
        b = whole(bg, n)
        high, low = halves(b - step * whole(qg, n) + beta * b)
        pg[n, 0:80] = high
        pg[n, 80:160] = low
        return total + op_term(pg, n)

    product = lax.fori_loop(0, 16, directions, zero)
    product = whole(pg, 0) * product
    product = jnp.concatenate([product, jnp.zeros((48, 256), F32)], axis=0)
    tiny[0] = dot(jnp.ones((8, 256), F32), product, NT, lax.Precision.HIGHEST)
    for i, j in others:
        at = (4 - i) % 4 * 4 + (4 - j) % 4
        send(tiny.at[0], tiny.at[at], s_t.at[at], r_t.at[at], plane_peer(i, j))

    first = 5 * (4 * y + x)
    line = lax.broadcasted_iota(jnp.int32, (16, 80), 0)
    column = lax.broadcasted_iota(jnp.int32, (16, 80), 1)
    pick = jnp.where((line < 5) & (column == line + first), 1.0, 0.0).astype(BF16)

    def picked(buf, n):
        return (dot(pick, buf[n, 0:80]) + dot(pick, buf[n, 80:160]))[0:8]

    bs = [picked(bg, n) for n in range(16)]
    ms = [picked(qg, n) for n in range(16)]

    def row_sum(parts):
        total = parts[0]
        for part in parts[1:]:
            total = total + part
        return jnp.sum(total, axis=1, keepdims=True)

    norm5 = row_sum([b * b for b in bs])
    step5 = norm5 / row_sum([b * m for b, m in zip(bs, ms)])
    rs = [b - step5 * m for b, m in zip(bs, ms)]
    next5 = row_sum([v * v for v in rs])
    ps = [v + next5 / norm5 * b for v, b in zip(rs, bs)]

    for i, j in reversed(others):
        at = 4 * i + j
        arrived(tiny.at[at], r_t.at[at])
    curv = tiny[0]
    for n in range(1, 16):
        curv = curv + tiny[n]
    line = lax.broadcasted_iota(jnp.int32, (8, 128), 0)
    column = lax.broadcasted_iota(jnp.int32, (8, 128), 1)
    curv = jnp.sum(jnp.where(column == line + first, curv, 0.0), axis=1, keepdims=True)
    step2 = next5 / curv
    for i in range(4):
        for j in range(4):
            n = 4 * i + j
            value = step5 * bs[n] + step2 * ps[n]
            col = pl.multiple_of(block_row(i, j) * 256, 256)
            out_ref[:, pl.ds(col, 256)] = value[0:5]
    for copy in sent:
        copy.wait_send()


def local(silo_grams, silo_weights):
    dma = pltpu.SemaphoreType.DMA
    scratch = [
        pltpu.VMEM((2, 256, 640), BF16),
        pltpu.VMEM((16, 2, 256, 256), F32),
        pltpu.VMEM((16, 512, 256), BF16),
        pltpu.VMEM((16, 512, 256), BF16),
        pltpu.VMEM((2, 4, 80, 512), BF16),
        pltpu.VMEM((16, 4, 80, 256), F32),
        pltpu.VMEM((16, 4, 80, 256), F32),
        pltpu.VMEM((16, 4, 80, 256), F32),
        pltpu.VMEM((2, 2, 4, 80, 256), F32),
        pltpu.VMEM((2, 4, 4, 80, 256), F32),
        pltpu.VMEM((3, 4, 80, 256), F32),
        pltpu.VMEM((3, 80, 256), F32),
        pltpu.VMEM((16, 256, 256), F32),
        pltpu.VMEM((8, 256, 256), F32),
        pltpu.VMEM((2, 256, 256), F32),
        pltpu.VMEM((2, 2, 256, 256), F32),
        pltpu.VMEM((16, 2, 256, 256), BF16),
        pltpu.VMEM((16, 160, 256), BF16),
        pltpu.VMEM((16, 160, 256), BF16),
        pltpu.VMEM((16, 160, 256), BF16),
        pltpu.VMEM((16, 8, 128), F32),
    ]
    counts = [1, 16, 5, 5, 8, 8, 6, 6, 3, 3, 1, 1, 6, 6, 4, 4, 5, 5, 16, 16, 16, 16, 16, 16]
    scratch += [dma((n,)) for n in counts]
    return pl.pallas_call(
        kernel,
        out_shape=jax.ShapeDtypeStruct((5, 4096), F32),
        in_specs=[pl.BlockSpec(memory_space=pl.ANY)] * 2,
        out_specs=pl.BlockSpec(memory_space=pltpu.VMEM),
        scratch_shapes=scratch,
        compiler_params=pltpu.CompilerParams(collective_id=0, has_side_effects=True, vmem_limit_bytes=62 << 20),
        cost_estimate=pl.CostEstimate(flops=6_500_000_000, bytes_accessed=9_200_000, transcendentals=0),
    )(silo_grams, silo_weights)


def solution(mesh):
    torus = Mesh(mesh.devices.reshape(4, 2, 4, 4), AXES)
    silo, row = ("z", "core"), ("y", "x")
    in_specs = (P(silo, row, None), P(silo, row, None))
    out_specs = P(silo + row, None)
    return jax.shard_map(local, mesh=torus, in_specs=in_specs, out_specs=out_specs, check_vma=False)
```

time: 125 us -> 102 us (0.82)
  the two profiles are of different devices: /device:TPU:1 before, /device:TPU:0 now
where the time goes in v2:
time: 102 us
  Pallas kernels  101 us (99%)
  local copies, waits for them, and re-layouts  1.57 us (2%)
    pallas_call x1, Pallas kernels, local(): pl.pallas_call(kernel, out_shape=jax.ShapeDtypeStruct((5, 4096), F32), in...  101 us

profile of v2, /device:TPU:0, one launch (start us, length us, event | category | flops | bytes accessed | tf_op | source)
XLA Modules:
  0.0 102.1 jit_solution(3748311591168113939)
XLA Ops:
  0.0 100.5 %shard_map.28 = f32[5,4096]{1,0:T(8,128)} custom-call(f32[2,256,4096]{2,1,0:T(8,128)} %g_hbm.1, bf16[2,256,640]{2,1,0:T(8,128)(2,1)} %w_hbm.1), custom_call_target="tpu_custom_call" | custom-call | flops 6499999744 | bytes 9200000 | tf_op jit(solution)/shard_map/pallas_call | solution.py:423
  100.5 1.6 %copy.4 = f32[5,4096]{1,0:T(8,128)} copy(f32[5,4096]{1,0:T(8,128)} %shard_map.28) | data formatting | bytes 163840

commit v3 on v2

--- a/solution.py
+++ b/solution.py
@@ -27,10 +27,10 @@
 def kernel(
     g_hbm, w_hbm, out_ref,
     w_raw, g, gh, gl, wt, p, q, r, far, near, second, third,
-    ap, a_sib, a_far, a_near, a_op, bg, qg, pg, tiny,
+    ap, a_sib, a_far, a_near, a_op, bg, qg, pg, five_out, five_in, tiny,
     w_sem, load_sem, s_sib, r_sib, s_one, r_one, s_two, r_two, s_z, r_z,
     s_asib, r_asib, s_ars, r_ars, s_aag, r_aag, s_afw, r_afw,
-    s_b, r_b, s_q, r_q, s_t, r_t,
+    s_b, r_b, s_q, r_q, s_f, r_f, s_t, r_t,
 ):
     z, k, y, x = (lax.axis_index(a) for a in AXES)
 
@@ -74,7 +74,7 @@
         col = pl.multiple_of(block_row(i, j) * 256, 256)
         return pltpu.make_async_copy(g_hbm.at[:, :, pl.ds(col, 256)], g.at[4 * i + j], load_sem.at[4 * i + j])
 
-    early = [(i, 2) for i in range(4)] + [(2, j) for j in (0, 1, 3)]
+    early = [(0, 2), (1, 2), (2, 0), (2, 1), (2, 2), (3, 2), (2, 3)]
     late = [(i, j) for j in (1, 3) for i in (0, 1, 3)] + [(1, 0), (3, 0), (0, 0)]
     for i, j in early + late:
         load(i, j).start()
@@ -92,13 +92,14 @@
     for s in range(8):
         wt[s % 2, lax.rem(s // 2 + 4 - z, 4)] = flipped[s * 80 : (s + 1) * 80]
 
+    def add_silos(i, j):
+        load(i, j).wait()
+        ap[canon(i, j)] = g[4 * i + j, 0] + g[4 * i + j, 1]
+
     def split(i, j):
-        load(i, j).wait()
-        value = g[4 * i + j]
-        high, low = halves(value)
+        high, low = halves(g[4 * i + j])
         gh[4 * i + j] = high.reshape(512, 256)
         gl[4 * i + j] = low.reshape(512, 256)
-        ap[canon(i, j)] = value[0] + value[1]
 
     def tile(core, slot):
         w = wt[core].reshape(320, 512)
@@ -109,7 +110,11 @@
             step(n)
             return carry
 
-        lax.fori_loop(0, count, body, 0)
+        if count == 2:
+            step(0)
+            step(1)
+        else:
+            lax.fori_loop(0, count, body, 0)
 
     def for_sibling(m, lo, count, sem):
         def step(n):
@@ -136,29 +141,50 @@
 
     up, down = plane_peer(1, 0), plane_peer(3, 0)
 
-    split(0, 2)
-    split(1, 2)
+    def prepare(*blocks):
+        for block in blocks:
+            add_silos(*block)
+            split(*block)
+
+    prepare(early[0], early[1])
     pl.semaphore_wait(barrier, 19)
     for_sibling(2, 0, 2, 0)
-    split(2, 2)
-    split(3, 2)
+    prepare(early[2], early[3])
+    for_self(2, 0, 2)
+    prepare(early[4], early[5])
     for_sibling(2, 2, 2, 1)
-    split(2, 0)
-    split(2, 1)
-    for_self(2, 0, 2)
     add_sibling(2, 0, 2, 0)
     send(p.at[pl.ds(8, 2)], far.at[0], s_one.at[0], r_one.at[0], up)
-    split(2, 3)
+    prepare(early[6])
     for_self(2, 2, 2)
+
+    for block in late:
+        add_silos(*block)
+    mine, theirs = pl.ds(8 * k, 8), pl.ds(8 * (1 - k), 8)
+    send(ap.at[theirs], a_sib, s_asib.at[0], r_asib.at[0], sibling)
     add_sibling(2, 2, 2, 1)
     send(p.at[pl.ds(10, 2)], far.at[1], s_one.at[1], r_one.at[1], down)
-
-    for i, j in late:
-        split(i, j)
-    mine, theirs = pl.ds(8 * k, 8), pl.ds(8 * (1 - k), 8)
-    send(ap.at[theirs], a_sib, s_asib.at[0], r_asib.at[0], sibling)
-
+    for block in late[:3]:
+        split(*block)
     for_sibling(1, 0, 4, 2)
+    arrived(a_sib, r_asib.at[0])
+
+    def add_op(n):
+        a_sib[n] += ap[8 * k + n]
+
+    loop(8, add_op)
+
+    def quarter(d, n):
+        return 2 * lax.rem(z + d, 4) + n
+
+    z_up, z_down = z_peer(1), z_peer(3)
+    send(a_sib.at[quarter(2, 0)], a_far.at[0], s_ars.at[0], r_ars.at[0], z_up)
+    send(a_sib.at[quarter(2, 1)], a_far.at[1], s_ars.at[1], r_ars.at[1], z_down)
+    send(a_sib.at[quarter(1, 1)], a_near.at[0, 1], s_ars.at[2], r_ars.at[2], z_up)
+    send(a_sib.at[quarter(3, 0)], a_near.at[1, 0], s_ars.at[3], r_ars.at[3], z_down)
+
+    for block in late[3:]:
+        split(*block)
     for_self(1, 0, 4)
     for_sibling(3, 0, 4, 3)
     add_sibling(1, 0, 4, 2)
@@ -166,22 +192,6 @@
     for_self(3, 0, 4)
     add_sibling(3, 0, 4, 3)
     send(p.at[pl.ds(12, 2)], near.at[1, pl.ds(0, 2)], s_one.at[3], r_one.at[3], down)
-
-    arrived(a_sib, r_asib.at[0])
-
-    def add_op(n):
-        a_sib[n] += ap[8 * k + n]
-
-    loop(8, add_op)
-
-    def quarter(d, n):
-        return 2 * lax.rem(z + d, 4) + n
-
-    z_up, z_down = z_peer(1), z_peer(3)
-    send(a_sib.at[quarter(2, 0)], a_far.at[0], s_ars.at[0], r_ars.at[0], z_up)
-    send(a_sib.at[quarter(2, 1)], a_far.at[1], s_ars.at[1], r_ars.at[1], z_down)
-    send(a_sib.at[quarter(1, 1)], a_near.at[0, 1], s_ars.at[2], r_ars.at[2], z_up)
-    send(a_sib.at[quarter(3, 0)], a_near.at[1, 0], s_ars.at[3], r_ars.at[3], z_down)
     for_sibling(0, 0, 4, 4)
     for_self(0, 0, 4)
     add_sibling(0, 0, 4, 4)
@@ -217,28 +227,30 @@
     arrived(near.at[1, 2], r_one.at[6])
     whole_sum(2)
     second_axis(2)
+
+    arrived(a_near.at[0, 1], r_ars.at[2])
+    arrived(a_near.at[1, 0], r_ars.at[3])
+    arrived(a_near.at[0, 0], r_ars.at[4])
+    arrived(a_near.at[1, 1], r_ars.at[5])
+
+    def pass_op(at, ssem, rsem, device):
+        send(a_op.at[at], a_op.at[at], ssem, rsem, device)
+
+    own = 8 * k + quarter(0, 0)
+    for n in range(2):
+        high, low = halves(a_sib[quarter(0, n)] + a_near[0, n] + a_near[1, n])
+        a_op[own + n, 0] = high
+        a_op[own + n, 1] = low
+    pass_op(own, s_aag.at[0], r_aag.at[0], z_up)
+    pass_op(own + 1, s_aag.at[1], r_aag.at[1], z_down)
+    pass_op(own + 1, s_aag.at[2], r_aag.at[2], z_up)
+    pass_op(own, s_aag.at[3], r_aag.at[3], z_down)
+
     arrived(near.at[1, 3], r_one.at[7])
     whole_sum(3)
     second_axis(3)
     arrived(near.at[0, 0], r_one.at[4])
     whole_sum(0)
-
-    arrived(a_near.at[0, 1], r_ars.at[2])
-    arrived(a_near.at[1, 0], r_ars.at[3])
-    arrived(a_near.at[0, 0], r_ars.at[4])
-    arrived(a_near.at[1, 1], r_ars.at[5])
-
-    def op_rows(d):
-        return pl.ds(8 * k + quarter(d, 0), 2)
-
-    own = 8 * k + quarter(0, 0)
-    for n in range(2):
-        high, low = halves(a_sib[quarter(0, n)] + a_near[0, n] + a_near[1, n])
-        a_op[own + n, 0] = high
-        a_op[own + n, 1] = low
-    send(a_op.at[op_rows(0)], a_op.at[op_rows(0)], s_aag.at[0], r_aag.at[0], z_up)
-    send(a_op.at[op_rows(0)], a_op.at[op_rows(0)], s_aag.at[1], r_aag.at[1], z_down)
-    send(a_op.at[op_rows(0)], a_op.at[op_rows(0)], s_afw.at[0], r_afw.at[0], sibling)
 
     for d in NEAR:
         arrived(second.at[3 - d, pl.ds(1, 3)], r_two.at[3 - d])
@@ -249,23 +261,19 @@
         arrived(second.at[3 - d, 0], r_two.at[6 - d])
     right = p[0, 0] + second[0, 0] + second[1, 0] + second[2, 0]
 
-    arrived(a_op.at[op_rows(3)], r_aag.at[0])
-    at = 8 * k + quarter(3, 0)
-    send(a_op.at[at], a_op.at[at], s_aag.at[2], r_aag.at[2], z_up)
-    send(a_op.at[op_rows(3)], a_op.at[op_rows(3)], s_afw.at[1], r_afw.at[1], sibling)
-    arrived(a_op.at[op_rows(1)], r_aag.at[1])
-    at = 8 * k + quarter(1, 1)
-    send(a_op.at[at], a_op.at[at], s_aag.at[3], r_aag.at[3], z_down)
-    send(a_op.at[op_rows(1)], a_op.at[op_rows(1)], s_afw.at[2], r_afw.at[2], sibling)
+    below, above, across = (8 * k + quarter(d, 0) for d in (3, 1, 2))
+    arrived(a_op.at[below], r_aag.at[0])
+    pass_op(below, s_aag.at[4], r_aag.at[4], z_up)
+    arrived(a_op.at[above + 1], r_aag.at[1])
+    pass_op(above + 1, s_aag.at[5], r_aag.at[5], z_down)
+    for n in range(2):
+        pass_op(own + n, s_afw.at[n], r_afw.at[n], sibling)
 
     for d in NEAR:
         arrived(third.at[3 - d], r_z.at[3 - d])
     right = right + third[0] + third[1] + third[2]
 
-    def spread(buf, value, ss, rs):
-        high, low = halves(value)
-        buf[0, 0:80] = high
-        buf[0, 80:160] = low
+    def spread(buf, ss, rs):
         for d in NEAR:
             send(buf.at[0], buf.at[16 - 4 * d], ss.at[16 - 4 * d], rs.at[16 - 4 * d], plane_peer(d, 0))
         for d in NEAR:
@@ -287,79 +295,95 @@
                 arrived(buf.at[at], rs.at[at])
                 use(at)
 
-    def whole(buf, slot):
-        return buf[slot, 0:80].astype(F32) + buf[slot, 80:160].astype(F32)
-
-    def op_term(buf, n):
+    def right_block(n):
+        return bg[n, 0:80].astype(F32) + bg[n, 80:160].astype(F32)
+
+    high, low = halves(right)
+    bg[0, 0:80] = high
+    bg[0, 80:160] = low
+    spread(bg, s_b, r_b)
+    pass_on(bg, s_b, r_b)
+
+    for at, n in ((below, 0), (above + 1, 1), (below + 1, 2), (above, 3), (across, 4), (across + 1, 5)):
+        if n > 1:
+            arrived(a_op.at[at], r_aag.at[n])
+        pass_op(at, s_afw.at[2 + n], r_afw.at[2 + n], sibling)
+    other = 8 * (1 - 2 * k)
+    for n, at in enumerate((own, own + 1, below, above + 1, below + 1, above, across, across + 1)):
+        arrived(a_op.at[at + other], r_afw.at[n])
+
+    zero = jnp.zeros((80, 256), F32)
+    total = [zero, zero]
+
+    def use_right(n):
         at = canon(n // 4, n % 4)
-        wide = dot(buf[n], a_op[at, 0], NT)
-        return wide[0:80] + wide[80:160] + dot(buf[n, 0:80], a_op[at, 1], NT)
-
-    zero = jnp.zeros((80, 256), F32)
-    spread(bg, right, s_b, r_b)
-    pass_on(bg, s_b, r_b)
-
-    for n in range(2):
-        at = 8 * k + quarter(2, n)
-        arrived(a_op.at[at], r_aag.at[2 + n])
-        send(a_op.at[at], a_op.at[at], s_afw.at[3 + n], r_afw.at[3 + n], sibling)
-    theirs = 8 * (1 - k)
-    for n, d in enumerate((0, 3, 1)):
-        arrived(a_op.at[pl.ds(theirs + quarter(d, 0), 2)], r_afw.at[n])
-    for n in range(2):
-        arrived(a_op.at[theirs + quarter(2, n)], r_afw.at[3 + n])
-
-    total = [zero, zero]
-
-    def use_right(n):
-        total[0] = total[0] + op_term(bg, n)
-        b = whole(bg, n)
+        wide = dot(bg[n], a_op[at, 0], NT)
+        total[0] = total[0] + wide[0:80] + wide[80:160] + dot(bg[n, 0:80], a_op[at, 1], NT)
+        b = right_block(n)
         total[1] = total[1] + b * b
 
     collect(bg, r_b, use_right)
     mapped, norm = total
     norm = jnp.sum(norm, axis=1, keepdims=True)
-    spread(qg, mapped, s_q, r_q)
+
+    high, low = halves(mapped)
+    qg[0] = high
+    spread(qg, s_q, r_q)
     pass_on(qg, s_q, r_q)
-    total = [zero]
-
-    def use_mapped(n):
-        total[0] = total[0] + whole(bg, n) * whole(qg, n)
-
-    collect(qg, r_q, use_mapped)
-    step = norm / jnp.sum(total[0], axis=1, keepdims=True)
-
-    def residuals(n, total):
-        res = whole(bg, n) - step * whole(qg, n)
-        return total + res * res
-
-    beta = jnp.sum(lax.fori_loop(0, 16, residuals, zero), axis=1, keepdims=True) / norm
-
-    def directions(n, total):
-        b = whole(bg, n)
-        high, low = halves(b - step * whole(qg, n) + beta * b)
-        pg[n, 0:80] = high
-        pg[n, 80:160] = low
-        return total + op_term(pg, n)
-
-    product = lax.fori_loop(0, 16, directions, zero)
-    product = whole(pg, 0) * product
-    product = jnp.concatenate([product, jnp.zeros((48, 256), F32)], axis=0)
-    tiny[0] = dot(jnp.ones((8, 256), F32), product, NT, lax.Precision.HIGHEST)
+
+    line = lax.broadcasted_iota(jnp.int32, (128, 80), 0)
+    column = lax.broadcasted_iota(jnp.int32, (128, 80), 1)
+    slot, line = lax.shift_right_logical(line, 3), line & 7
+    dx, dy = dxy(lax.shift_right_logical(slot, 2), slot & 3)
+    row = ((y + dy) & 3) * 4 + ((x + dx) & 3)
+    pick = jnp.where((line < 5) & (column == line + 5 * row), 1.0, 0.0).astype(BF16)
+    five_out[...] = (dot(pick, high) + dot(pick, low)).reshape(16, 8, 256)
     for i, j in others:
         at = (4 - i) % 4 * 4 + (4 - j) % 4
-        send(tiny.at[0], tiny.at[at], s_t.at[at], r_t.at[at], plane_peer(i, j))
+        send(five_out.at[4 * i + j], five_in.at[at], s_f.at[at], r_f.at[at], plane_peer(i, j))
 
     first = 5 * (4 * y + x)
     line = lax.broadcasted_iota(jnp.int32, (16, 80), 0)
     column = lax.broadcasted_iota(jnp.int32, (16, 80), 1)
     pick = jnp.where((line < 5) & (column == line + first), 1.0, 0.0).astype(BF16)
-
-    def picked(buf, n):
-        return (dot(pick, buf[n, 0:80]) + dot(pick, buf[n, 80:160]))[0:8]
-
-    bs = [picked(bg, n) for n in range(16)]
-    ms = [picked(qg, n) for n in range(16)]
+    bs = [(dot(pick, bg[n, 0:80]) + dot(pick, bg[n, 80:160]))[0:8] for n in range(16)]
+
+    total = [zero]
+
+    def use_mapped(n):
+        total[0] = total[0] + right_block(n) * qg[n].astype(F32)
+
+    collect(qg, r_q, use_mapped)
+    step = norm / jnp.sum(total[0], axis=1, keepdims=True)
+
+    def residuals(n, total):
+        res = right_block(n) - step * qg[n].astype(F32)
+        return total + res * res
+
+    beta = jnp.sum(lax.fori_loop(0, 16, residuals, zero), axis=1, keepdims=True) / norm
+
+    def directions(n, total):
+        b = right_block(n)
+        close = (b - step * qg[n].astype(F32) + beta * b).astype(BF16)
+        at = canon(n // 4, n % 4)
+
+        @pl.when(n == 0)
+        def _():
+            pg[...] = close
+
+        return total + dot(close, a_op[at, 0], NT) + dot(close, a_op[at, 1], NT)
+
+    image = lax.fori_loop(0, 16, directions, zero)
+    products = [right_block(0) * image, mapped * image, pg[...].astype(F32) * image, jnp.zeros((16, 256), F32)]
+    tiny[0] = dot(jnp.ones((8, 256), F32), jnp.concatenate(products, axis=0), NT, lax.Precision.HIGHEST)
+    for i, j in others:
+        at = (4 - i) % 4 * 4 + (4 - j) % 4
+        send(tiny.at[0], tiny.at[at], s_t.at[at], r_t.at[at], plane_peer(i, j))
+
+    for i, j in reversed(others):
+        at = 4 * i + j
+        arrived(five_in.at[at], r_f.at[at])
+    ms = [five_out[0]] + [five_in[n] for n in range(1, 16)]
 
     def row_sum(parts):
         total = parts[0]
@@ -371,17 +395,22 @@
     step5 = norm5 / row_sum([b * m for b, m in zip(bs, ms)])
     rs = [b - step5 * m for b, m in zip(bs, ms)]
     next5 = row_sum([v * v for v in rs])
-    ps = [v + next5 / norm5 * b for v, b in zip(rs, bs)]
+    beta5 = next5 / norm5
+    ps = [v + beta5 * b for v, b in zip(rs, bs)]
 
     for i, j in reversed(others):
         at = 4 * i + j
         arrived(tiny.at[at], r_t.at[at])
-    curv = tiny[0]
+    sums = tiny[0]
     for n in range(1, 16):
-        curv = curv + tiny[n]
-    line = lax.broadcasted_iota(jnp.int32, (8, 128), 0)
-    column = lax.broadcasted_iota(jnp.int32, (8, 128), 1)
-    curv = jnp.sum(jnp.where(column == line + first, curv, 0.0), axis=1, keepdims=True)
+        sums = sums + tiny[n]
+    line = lax.broadcasted_iota(jnp.int32, (8, 256), 0)
+    column = lax.broadcasted_iota(jnp.int32, (8, 256), 1)
+
+    def five(start):
+        return jnp.sum(jnp.where(column == line + (first + start), sums, 0.0), axis=1, keepdims=True)
+
+    curv = 2.0 * ((1.0 + beta5) * five(0) - step5 * five(80)) - five(160)
     step2 = next5 / curv
     for i in range(4):
         for j in range(4):
@@ -414,11 +443,13 @@
         pltpu.VMEM((2, 2, 256, 256), F32),
         pltpu.VMEM((16, 2, 256, 256), BF16),
         pltpu.VMEM((16, 160, 256), BF16),
-        pltpu.VMEM((16, 160, 256), BF16),
-        pltpu.VMEM((16, 160, 256), BF16),
-        pltpu.VMEM((16, 8, 128), F32),
+        pltpu.VMEM((16, 80, 256), BF16),
+        pltpu.VMEM((80, 256), BF16),
+        pltpu.VMEM((16, 8, 256), F32),
+        pltpu.VMEM((16, 8, 256), F32),
+        pltpu.VMEM((16, 8, 256), F32),
     ]
-    counts = [1, 16, 5, 5, 8, 8, 6, 6, 3, 3, 1, 1, 6, 6, 4, 4, 5, 5, 16, 16, 16, 16, 16, 16]
+    counts = [1, 16, 5, 5, 8, 8, 6, 6, 3, 3, 1, 1, 6, 6, 6, 6, 8, 8, 16, 16, 16, 16, 16, 16, 16, 16]
     scratch += [dma((n,)) for n in counts]
     return pl.pallas_call(
         kernel,

time: 102 us -> 91.3 us (0.90)
  Pallas kernels: 101 us -> 89.6 us
    pallas_call x1, Pallas kernels: 101 us -> 89.6 us  [local(): pl.pallas_call(kernel, out_shape=jax.ShapeDtypeStruct((5, 4096), F32), in...]
where the time goes in v3:
time: 91.3 us; the launch traced here: 91.2 us
  Pallas kernels  89.6 us (98%)
  local copies, waits for them, and re-layouts  1.57 us (2%)
    pallas_call x1, Pallas kernels, local(): pl.pallas_call(kernel, out_shape=jax.ShapeDtypeStruct((5, 4096), F32), in...  89.6 us

profile of v3, /device:TPU:0, one launch (start us, length us, event | category | flops | bytes accessed | tf_op | source)
XLA Modules:
  0.0 91.2 jit_solution(13667221029688028090)
XLA Ops:
  0.0 89.6 %shard_map.28 = f32[5,4096]{1,0:T(8,128)} custom-call(f32[2,256,4096]{2,1,0:T(8,128)} %g_hbm.1, bf16[2,256,640]{2,1,0:T(8,128)(2,1)} %w_hbm.1), custom_call_target="tpu_custom_call" | custom-call | flops 6499999744 | bytes 9200000 | tf_op jit(solution)/shard_map/pallas_call | solution.py:454
  89.6 1.6 %copy.4 = f32[5,4096]{1,0:T(8,128)} copy(f32[5,4096]{1,0:T(8,128)} %shard_map.28) | data formatting | bytes 163840

commit v4 on v3

--- a/solution.py
+++ b/solution.py
@@ -26,8 +26,8 @@
 
 def kernel(
     g_hbm, w_hbm, out_ref,
-    w_raw, g, gh, gl, wt, p, q, r, far, near, second, third,
-    ap, a_sib, a_far, a_near, a_op, bg, qg, pg, five_out, five_in, tiny,
+    w_raw, g, wt, p, q, r, far, near, second, third,
+    ap, a_sib, a_far, a_near, a_op, bg, qg, five_out, five_in, tiny,
     w_sem, load_sem, s_sib, r_sib, s_one, r_one, s_two, r_two, s_z, r_z,
     s_asib, r_asib, s_ars, r_ars, s_aag, r_aag, s_afw, r_afw,
     s_b, r_b, s_q, r_q, s_f, r_f, s_t, r_t,
@@ -74,9 +74,9 @@
         col = pl.multiple_of(block_row(i, j) * 256, 256)
         return pltpu.make_async_copy(g_hbm.at[:, :, pl.ds(col, 256)], g.at[4 * i + j], load_sem.at[4 * i + j])
 
-    early = [(0, 2), (1, 2), (2, 0), (2, 1), (2, 2), (3, 2), (2, 3)]
-    late = [(i, j) for j in (1, 3) for i in (0, 1, 3)] + [(1, 0), (3, 0), (0, 0)]
-    for i, j in early + late:
+    blocks = [(2, 2), (1, 2), (2, 1), (2, 0), (0, 2), (2, 3), (3, 2), (1, 3), (3, 1), (3, 0), (0, 3)]
+    blocks += [(1, 1), (1, 0), (0, 1), (3, 3), (0, 0)]
+    for i, j in blocks:
         load(i, j).start()
 
     barrier = pltpu.get_barrier_semaphore()
@@ -90,121 +90,109 @@
     weights.wait()
     flipped = w_raw[...].reshape(512, 640).astype(F32).T.astype(BF16)
     for s in range(8):
-        wt[s % 2, lax.rem(s // 2 + 4 - z, 4)] = flipped[s * 80 : (s + 1) * 80]
-
-    def add_silos(i, j):
-        load(i, j).wait()
-        ap[canon(i, j)] = g[4 * i + j, 0] + g[4 * i + j, 1]
-
-    def split(i, j):
-        high, low = halves(g[4 * i + j])
-        gh[4 * i + j] = high.reshape(512, 256)
-        gl[4 * i + j] = low.reshape(512, 256)
-
-    def tile(core, slot):
-        w = wt[core].reshape(320, 512)
-        return (dot(w, gh[slot]) + dot(w, gl[slot])).reshape(4, 80, 256)
-
-    def loop(count, step):
-        def body(n, carry):
-            step(n)
-            return carry
-
-        if count == 2:
-            step(0)
-            step(1)
-        else:
-            lax.fori_loop(0, count, body, 0)
-
-    def for_sibling(m, lo, count, sem):
-        def step(n):
-            q[4 * m + lo + n] = tile(1 - k, 4 * (lo + n) + m)
-
-        loop(count, step)
-        rows = pl.ds(4 * m + lo, count)
+        wt[lax.rem(s + k, 2), lax.rem(s // 2 + 4 - z, 4)] = flipped[s * 80 : (s + 1) * 80]
+
+    summed = []
+
+    def add_silos(count):
+        for i, j in blocks[len(summed) : count]:
+            load(i, j).wait()
+            ap[canon(i, j)] = g[4 * i + j, 0] + g[4 * i + j, 1]
+            summed.append((i, j))
+
+    def tiles(lo, hi):
+        add_silos(hi)
+        for i, j in blocks[lo:hi]:
+            high, low = halves(g[4 * i + j])
+            w = wt[...].reshape(640, 512)
+            both = dot(w, high.reshape(512, 256)) + dot(w, low.reshape(512, 256))
+            p[4 * i + j] = both[:320].reshape(4, 80, 256)
+            q[4 * j + i] = both[320:].reshape(4, 80, 256)
+
+    def to_sibling(lo, count, sem):
+        rows = pl.ds(lo, count)
         send(q.at[rows], r.at[rows], s_sib.at[sem], r_sib.at[sem], sibling)
 
-    def for_self(m, lo, count):
-        def step(n):
-            p[4 * m + lo + n] = tile(k, 4 * m + lo + n)
-
-        loop(count, step)
-
-    def add_sibling(m, lo, count, sem):
-        rows = pl.ds(4 * m + lo, count)
+    def add_sibling(lo, count, sem):
+        rows = pl.ds(lo, count)
         arrived(r.at[rows], r_sib.at[sem])
-
-        def step(n):
-            p[4 * m + lo + n] += r[4 * m + lo + n]
-
-        loop(count, step)
-
-    up, down = plane_peer(1, 0), plane_peer(3, 0)
-
-    def prepare(*blocks):
-        for block in blocks:
-            add_silos(*block)
-            split(*block)
-
-    prepare(early[0], early[1])
-    pl.semaphore_wait(barrier, 19)
-    for_sibling(2, 0, 2, 0)
-    prepare(early[2], early[3])
-    for_self(2, 0, 2)
-    prepare(early[4], early[5])
-    for_sibling(2, 2, 2, 1)
-    add_sibling(2, 0, 2, 0)
-    send(p.at[pl.ds(8, 2)], far.at[0], s_one.at[0], r_one.at[0], up)
-    prepare(early[6])
-    for_self(2, 2, 2)
-
-    for block in late:
-        add_silos(*block)
-    mine, theirs = pl.ds(8 * k, 8), pl.ds(8 * (1 - k), 8)
-    send(ap.at[theirs], a_sib, s_asib.at[0], r_asib.at[0], sibling)
-    add_sibling(2, 2, 2, 1)
-    send(p.at[pl.ds(10, 2)], far.at[1], s_one.at[1], r_one.at[1], down)
-    for block in late[:3]:
-        split(*block)
-    for_sibling(1, 0, 4, 2)
-    arrived(a_sib, r_asib.at[0])
-
-    def add_op(n):
-        a_sib[n] += ap[8 * k + n]
-
-    loop(8, add_op)
+        for n in range(lo, lo + count):
+            p[n] += r[n]
 
     def quarter(d, n):
         return 2 * lax.rem(z + d, 4) + n
 
+    up, down = plane_peer(1, 0), plane_peer(3, 0)
     z_up, z_down = z_peer(1), z_peer(3)
+
+    tiles(0, 3)
+    pl.semaphore_wait(barrier, 19)
+    to_sibling(9, 2, 0)
+    tiles(3, 5)
+    to_sibling(8, 1, 1)
+    add_sibling(9, 2, 0)
+    send(p.at[9], far.at[0, 1], s_one.at[0], r_one.at[0], up)
+    send(p.at[10], far.at[1, 0], s_one.at[1], r_one.at[1], down)
+
+    def op_to_sibling(d):
+        rows = pl.ds(quarter(d, 0), 2)
+        send(ap.at[pl.ds(8 * (1 - k) + quarter(d, 0), 2)], a_sib.at[rows], s_asib.at[d], r_asib.at[d], sibling)
+
+    def op_from_sibling(d):
+        arrived(a_sib.at[pl.ds(quarter(d, 0), 2)], r_asib.at[d])
+        for n in range(2):
+            a_sib[quarter(d, n)] += ap[8 * k + quarter(d, n)]
+
+    add_silos(16)
+    op_to_sibling(2)
+    tiles(5, 7)
+    to_sibling(11, 1, 2)
+    add_sibling(8, 1, 1)
+    send(p.at[8], far.at[0, 0], s_one.at[8], r_one.at[8], up)
+    op_from_sibling(2)
     send(a_sib.at[quarter(2, 0)], a_far.at[0], s_ars.at[0], r_ars.at[0], z_up)
     send(a_sib.at[quarter(2, 1)], a_far.at[1], s_ars.at[1], r_ars.at[1], z_down)
+    tiles(7, 9)
+    add_sibling(11, 1, 2)
+    send(p.at[11], far.at[1, 1], s_one.at[9], r_one.at[9], down)
+    tiles(9, 11)
+    to_sibling(6, 2, 3)
+    to_sibling(12, 2, 4)
+    op_to_sibling(1)
+    op_to_sibling(3)
+    tiles(11, 13)
+    add_sibling(6, 2, 3)
+    send(p.at[pl.ds(6, 2)], near.at[0, pl.ds(2, 2)], s_one.at[2], r_one.at[2], up)
+    add_sibling(12, 2, 4)
+    send(p.at[pl.ds(12, 2)], near.at[1, pl.ds(0, 2)], s_one.at[3], r_one.at[3], down)
+    tiles(13, 15)
+    to_sibling(4, 2, 5)
+    to_sibling(14, 2, 6)
+    op_from_sibling(1)
     send(a_sib.at[quarter(1, 1)], a_near.at[0, 1], s_ars.at[2], r_ars.at[2], z_up)
+    op_from_sibling(3)
     send(a_sib.at[quarter(3, 0)], a_near.at[1, 0], s_ars.at[3], r_ars.at[3], z_down)
-
-    for block in late[3:]:
-        split(*block)
-    for_self(1, 0, 4)
-    for_sibling(3, 0, 4, 3)
-    add_sibling(1, 0, 4, 2)
-    send(p.at[pl.ds(6, 2)], near.at[0, pl.ds(2, 2)], s_one.at[2], r_one.at[2], up)
-    for_self(3, 0, 4)
-    add_sibling(3, 0, 4, 3)
-    send(p.at[pl.ds(12, 2)], near.at[1, pl.ds(0, 2)], s_one.at[3], r_one.at[3], down)
-    for_sibling(0, 0, 4, 4)
-    for_self(0, 0, 4)
-    add_sibling(0, 0, 4, 4)
-
-    arrived(far.at[0], r_one.at[0])
-    for n in (1, 0):
+    tiles(15, 16)
+    to_sibling(0, 4, 7)
+    op_to_sibling(0)
+    add_sibling(4, 2, 5)
+    add_sibling(14, 2, 6)
+
+    def relay_up(n, sem):
+        arrived(far.at[0, n], r_one.at[sem])
         p[4 + n] += far[0, n]
         send(p.at[4 + n], near.at[0, n], s_one.at[4 + n], r_one.at[4 + n], up)
-    arrived(far.at[1], r_one.at[1])
-    for n in range(2):
+
+    def relay_down(n, sem):
+        arrived(far.at[1, n], r_one.at[sem])
         p[14 + n] += far[1, n]
         send(p.at[14 + n], near.at[1, 2 + n], s_one.at[6 + n], r_one.at[6 + n], down)
 
+    relay_up(1, 0)
+    relay_down(0, 1)
+    add_sibling(0, 4, 7)
+    relay_up(0, 8)
+    relay_down(1, 9)
     arrived(a_far.at[0], r_ars.at[0])
     a_sib[quarter(1, 0)] += a_far[0]
     send(a_sib.at[quarter(1, 0)], a_near.at[0, 0], s_ars.at[4], r_ars.at[4], z_up)
@@ -236,6 +224,7 @@
     def pass_op(at, ssem, rsem, device):
         send(a_op.at[at], a_op.at[at], ssem, rsem, device)
 
+    op_from_sibling(0)
     own = 8 * k + quarter(0, 0)
     for n in range(2):
         high, low = halves(a_sib[quarter(0, n)] + a_near[0, n] + a_near[1, n])
@@ -245,7 +234,6 @@
     pass_op(own + 1, s_aag.at[1], r_aag.at[1], z_down)
     pass_op(own + 1, s_aag.at[2], r_aag.at[2], z_up)
     pass_op(own, s_aag.at[3], r_aag.at[3], z_down)
-
     arrived(near.at[1, 3], r_one.at[7])
     whole_sum(3)
     second_axis(3)
@@ -261,14 +249,6 @@
         arrived(second.at[3 - d, 0], r_two.at[6 - d])
     right = p[0, 0] + second[0, 0] + second[1, 0] + second[2, 0]
 
-    below, above, across = (8 * k + quarter(d, 0) for d in (3, 1, 2))
-    arrived(a_op.at[below], r_aag.at[0])
-    pass_op(below, s_aag.at[4], r_aag.at[4], z_up)
-    arrived(a_op.at[above + 1], r_aag.at[1])
-    pass_op(above + 1, s_aag.at[5], r_aag.at[5], z_down)
-    for n in range(2):
-        pass_op(own + n, s_afw.at[n], r_afw.at[n], sibling)
-
     for d in NEAR:
         arrived(third.at[3 - d], r_z.at[3 - d])
     right = right + third[0] + third[1] + third[2]
@@ -302,6 +282,15 @@
     bg[0, 0:80] = high
     bg[0, 80:160] = low
     spread(bg, s_b, r_b)
+
+    below, above, across = (8 * k + quarter(d, 0) for d in (3, 1, 2))
+    arrived(a_op.at[below], r_aag.at[0])
+    pass_op(below, s_aag.at[4], r_aag.at[4], z_up)
+    arrived(a_op.at[above + 1], r_aag.at[1])
+    pass_op(above + 1, s_aag.at[5], r_aag.at[5], z_down)
+    for n in range(2):
+        pass_op(own + n, s_afw.at[n], r_afw.at[n], sibling)
+
     pass_on(bg, s_b, r_b)
 
     for at, n in ((below, 0), (above + 1, 1), (below + 1, 2), (above, 3), (across, 4), (across + 1, 5)):
@@ -348,33 +337,28 @@
     pick = jnp.where((line < 5) & (column == line + first), 1.0, 0.0).astype(BF16)
     bs = [(dot(pick, bg[n, 0:80]) + dot(pick, bg[n, 80:160]))[0:8] for n in range(16)]
 
-    total = [zero]
+    total = [zero, zero]
 
     def use_mapped(n):
-        total[0] = total[0] + right_block(n) * qg[n].astype(F32)
+        m = qg[n].astype(F32)
+        total[0] = total[0] + right_block(n) * m
+        total[1] = total[1] + m * m
 
     collect(qg, r_q, use_mapped)
     step = norm / jnp.sum(total[0], axis=1, keepdims=True)
 
-    def residuals(n, total):
-        res = right_block(n) - step * qg[n].astype(F32)
-        return total + res * res
-
-    beta = jnp.sum(lax.fori_loop(0, 16, residuals, zero), axis=1, keepdims=True) / norm
-
-    def directions(n, total):
+    size = jnp.sum(total[1], axis=1, keepdims=True)
+    beta = jnp.maximum(step * step * size / norm - 1.0, 0.0)
+
+    image = zero
+    for n in range(16):
         b = right_block(n)
         close = (b - step * qg[n].astype(F32) + beta * b).astype(BF16)
         at = canon(n // 4, n % 4)
-
-        @pl.when(n == 0)
-        def _():
-            pg[...] = close
-
-        return total + dot(close, a_op[at, 0], NT) + dot(close, a_op[at, 1], NT)
-
-    image = lax.fori_loop(0, 16, directions, zero)
-    products = [right_block(0) * image, mapped * image, pg[...].astype(F32) * image, jnp.zeros((16, 256), F32)]
+        image = image + dot(close, a_op[at, 0], NT) + dot(close, a_op[at, 1], NT)
+        if n == 0:
+            mine = close.astype(F32)
+    products = [right_block(0) * image, mapped * image, mine * image, jnp.zeros((16, 256), F32)]
     tiny[0] = dot(jnp.ones((8, 256), F32), jnp.concatenate(products, axis=0), NT, lax.Precision.HIGHEST)
     for i, j in others:
         at = (4 - i) % 4 * 4 + (4 - j) % 4
@@ -427,8 +411,6 @@
     scratch = [
         pltpu.VMEM((2, 256, 640), BF16),
         pltpu.VMEM((16, 2, 256, 256), F32),
-        pltpu.VMEM((16, 512, 256), BF16),
-        pltpu.VMEM((16, 512, 256), BF16),
         pltpu.VMEM((2, 4, 80, 512), BF16),
         pltpu.VMEM((16, 4, 80, 256), F32),
         pltpu.VMEM((16, 4, 80, 256), F32),
@@ -444,12 +426,11 @@
         pltpu.VMEM((16, 2, 256, 256), BF16),
         pltpu.VMEM((16, 160, 256), BF16),
         pltpu.VMEM((16, 80, 256), BF16),
-        pltpu.VMEM((80, 256), BF16),
         pltpu.VMEM((16, 8, 256), F32),
         pltpu.VMEM((16, 8, 256), F32),
         pltpu.VMEM((16, 8, 256), F32),
     ]
-    counts = [1, 16, 5, 5, 8, 8, 6, 6, 3, 3, 1, 1, 6, 6, 6, 6, 8, 8, 16, 16, 16, 16, 16, 16, 16, 16]
+    counts = [1, 16, 8, 8, 10, 10, 6, 6, 3, 3, 4, 4, 6, 6, 6, 6, 8, 8, 16, 16, 16, 16, 16, 16, 16, 16]
     scratch += [dma((n,)) for n in counts]
     return pl.pallas_call(
         kernel,

time: 91.3 us -> 87.9 us (0.963)
  Pallas kernels: 89.6 us -> 86.2 us
    pallas_call x1, Pallas kernels: 89.6 us -> 86.2 us  [local(): pl.pallas_call(kernel, out_shape=jax.ShapeDtypeStruct((5, 4096), F32), in...]
where the time goes in v4:
time: 87.9 us; the launch traced here: 87.7 us
  Pallas kernels  86.2 us (98%)
  local copies, waits for them, and re-layouts  1.57 us (2%)
    pallas_call x1, Pallas kernels, local(): pl.pallas_call(kernel, out_shape=jax.ShapeDtypeStruct((5, 4096), F32), in...  86.2 us

profile of v4, /device:TPU:0, one launch (start us, length us, event | category | flops | bytes accessed | tf_op | source)
XLA Modules:
  0.0 87.7 jit_solution(12158938985856627177)
XLA Ops:
  0.0 86.2 %shard_map.28 = f32[5,4096]{1,0:T(8,128)} custom-call(f32[2,256,4096]{2,1,0:T(8,128)} %g_hbm.1, bf16[2,256,640]{2,1,0:T(8,128)(2,1)} %w_hbm.1), custom_call_target="tpu_custom_call" | custom-call | flops 6499999744 | bytes 9200000 | tf_op jit(solution)/shard_map/pallas_call | solution.py:435
  86.2 1.6 %copy.4 = f32[5,4096]{1,0:T(8,128)} copy(f32[5,4096]{1,0:T(8,128)} %shard_map.28) | data formatting | bytes 163840

commit v5 on v4

--- a/solution.py
+++ b/solution.py
@@ -27,10 +27,10 @@
 def kernel(
     g_hbm, w_hbm, out_ref,
     w_raw, g, wt, p, q, r, far, near, second, third,
-    ap, a_sib, a_far, a_near, a_op, bg, qg, five_out, five_in, tiny,
+    ap, a_sib, a_far, a_near, a_op, bg, bl, qg, acc, five_out, five_in, tiny,
     w_sem, load_sem, s_sib, r_sib, s_one, r_one, s_two, r_two, s_z, r_z,
     s_asib, r_asib, s_ars, r_ars, s_aag, r_aag, s_afw, r_afw,
-    s_b, r_b, s_q, r_q, s_f, r_f, s_t, r_t,
+    s_b, r_b, s_l, r_l, s_q, r_q, s_f, r_f, s_t, r_t,
 ):
     z, k, y, x = (lax.axis_index(a) for a in AXES)
 
@@ -276,11 +276,11 @@
                 use(at)
 
     def right_block(n):
-        return bg[n, 0:80].astype(F32) + bg[n, 80:160].astype(F32)
+        return bg[n].astype(F32) + bl[n].astype(F32)
 
     high, low = halves(right)
-    bg[0, 0:80] = high
-    bg[0, 80:160] = low
+    bg[0] = high
+    bl[0] = low
     spread(bg, s_b, r_b)
 
     below, above, across = (8 * k + quarter(d, 0) for d in (3, 1, 2))
@@ -292,6 +292,7 @@
         pass_op(own + n, s_afw.at[n], r_afw.at[n], sibling)
 
     pass_on(bg, s_b, r_b)
+    spread(bl, s_l, r_l)
 
     for at, n in ((below, 0), (above + 1, 1), (below + 1, 2), (above, 3), (across, 4), (across + 1, 5)):
         if n > 1:
@@ -302,23 +303,31 @@
         arrived(a_op.at[at + other], r_afw.at[n])
 
     zero = jnp.zeros((80, 256), F32)
-    total = [zero, zero]
-
-    def use_right(n):
+    total = [zero]
+
+    def use_high(n):
         at = canon(n // 4, n % 4)
-        wide = dot(bg[n], a_op[at, 0], NT)
-        total[0] = total[0] + wide[0:80] + wide[80:160] + dot(bg[n, 0:80], a_op[at, 1], NT)
+        total[0] = total[0] + dot(bg[n], a_op[at, 0], NT) + dot(bg[n], a_op[at, 1], NT)
+
+    collect(bg, r_b, use_high)
+    acc[...] = total[0]
+    qg[0] = total[0].astype(BF16)
+    spread(qg, s_q, r_q)
+    pass_on(bl, s_l, r_l)
+    pass_on(qg, s_q, r_q)
+
+    total = [zero]
+
+    def use_low(n):
+        total[0] = total[0] + dot(bl[n], a_op[canon(n // 4, n % 4), 0], NT)
+
+    collect(bl, r_l, use_low)
+    mapped = acc[...] + total[0]
+    norm = zero
+    for n in range(16):
         b = right_block(n)
-        total[1] = total[1] + b * b
-
-    collect(bg, r_b, use_right)
-    mapped, norm = total
+        norm = norm + b * b
     norm = jnp.sum(norm, axis=1, keepdims=True)
-
-    high, low = halves(mapped)
-    qg[0] = high
-    spread(qg, s_q, r_q)
-    pass_on(qg, s_q, r_q)
 
     line = lax.broadcasted_iota(jnp.int32, (128, 80), 0)
     column = lax.broadcasted_iota(jnp.int32, (128, 80), 1)
@@ -326,6 +335,7 @@
     dx, dy = dxy(lax.shift_right_logical(slot, 2), slot & 3)
     row = ((y + dy) & 3) * 4 + ((x + dx) & 3)
     pick = jnp.where((line < 5) & (column == line + 5 * row), 1.0, 0.0).astype(BF16)
+    high, low = halves(mapped)
     five_out[...] = (dot(pick, high) + dot(pick, low)).reshape(16, 8, 256)
     for i, j in others:
         at = (4 - i) % 4 * 4 + (4 - j) % 4
@@ -335,7 +345,7 @@
     line = lax.broadcasted_iota(jnp.int32, (16, 80), 0)
     column = lax.broadcasted_iota(jnp.int32, (16, 80), 1)
     pick = jnp.where((line < 5) & (column == line + first), 1.0, 0.0).astype(BF16)
-    bs = [(dot(pick, bg[n, 0:80]) + dot(pick, bg[n, 80:160]))[0:8] for n in range(16)]
+    bs = [(dot(pick, bg[n]) + dot(pick, bl[n]))[0:8] for n in range(16)]
 
     total = [zero, zero]
 
@@ -424,13 +434,15 @@
         pltpu.VMEM((2, 256, 256), F32),
         pltpu.VMEM((2, 2, 256, 256), F32),
         pltpu.VMEM((16, 2, 256, 256), BF16),
-        pltpu.VMEM((16, 160, 256), BF16),
         pltpu.VMEM((16, 80, 256), BF16),
+        pltpu.VMEM((16, 80, 256), BF16),
+        pltpu.VMEM((16, 80, 256), BF16),
+        pltpu.VMEM((80, 256), F32),
         pltpu.VMEM((16, 8, 256), F32),
         pltpu.VMEM((16, 8, 256), F32),
         pltpu.VMEM((16, 8, 256), F32),
     ]
-    counts = [1, 16, 8, 8, 10, 10, 6, 6, 3, 3, 4, 4, 6, 6, 6, 6, 8, 8, 16, 16, 16, 16, 16, 16, 16, 16]
+    counts = [1, 16, 8, 8, 10, 10, 6, 6, 3, 3, 4, 4, 6, 6, 6, 6, 8, 8, 16, 16, 16, 16, 16, 16, 16, 16, 16, 16]
     scratch += [dma((n,)) for n in counts]
     return pl.pallas_call(
         kernel,

time: 87.9 us -> 85 us (0.967)
  Pallas kernels: 86.2 us -> 83.3 us
    pallas_call x1, Pallas kernels: 86.2 us -> 83.3 us  [local(): pl.pallas_call(kernel, out_shape=jax.ShapeDtypeStruct((5, 4096), F32), in...]
where the time goes in v5:
time: 85 us; the launch traced here: 84.9 us
  Pallas kernels  83.3 us (98%)
  local copies, waits for them, and re-layouts  1.57 us (2%)
    pallas_call x1, Pallas kernels, local(): pl.pallas_call(kernel, out_shape=jax.ShapeDtypeStruct((5, 4096), F32), in...  83.3 us

profile of v5, /device:TPU:0, one launch (start us, length us, event | category | flops | bytes accessed | tf_op | source)
XLA Modules:
  0.0 84.9 jit_solution(7122119445780803903)
XLA Ops:
  0.0 83.3 %shard_map.28 = f32[5,4096]{1,0:T(8,128)} custom-call(f32[2,256,4096]{2,1,0:T(8,128)} %g_hbm.1, bf16[2,256,640]{2,1,0:T(8,128)(2,1)} %w_hbm.1), custom_call_target="tpu_custom_call" | custom-call | flops 6499999744 | bytes 9200000 | tf_op jit(solution)/shard_map/pallas_call | solution.py:447
  83.3 1.6 %copy.4 = f32[5,4096]{1,0:T(8,128)} copy(f32[5,4096]{1,0:T(8,128)} %shard_map.28) | data formatting | bytes 163840

commit v6 on v5

--- a/solution.py
+++ b/solution.py
@@ -76,7 +76,7 @@
 
     blocks = [(2, 2), (1, 2), (2, 1), (2, 0), (0, 2), (2, 3), (3, 2), (1, 3), (3, 1), (3, 0), (0, 3)]
     blocks += [(1, 1), (1, 0), (0, 1), (3, 3), (0, 0)]
-    for i, j in blocks:
+    for i, j in blocks[:5]:
         load(i, j).start()
 
     barrier = pltpu.get_barrier_semaphore()
@@ -125,6 +125,8 @@
     up, down = plane_peer(1, 0), plane_peer(3, 0)
     z_up, z_down = z_peer(1), z_peer(3)
 
+    for i, j in blocks[5:]:
+        load(i, j).start()
     tiles(0, 3)
     pl.semaphore_wait(barrier, 19)
     to_sibling(9, 2, 0)

time: 85 us -> 83.6 us (0.984)
  Pallas kernels: 83.3 us -> 81.5 us
    pallas_call x1, Pallas kernels: 83.3 us -> 81.5 us  [local(): pl.pallas_call(kernel, out_shape=jax.ShapeDtypeStruct((5, 4096), F32), in...]
where the time goes in v6:
time: 83.6 us; the launch traced here: 83.1 us
  Pallas kernels  81.5 us (97%)
  local copies, waits for them, and re-layouts  1.57 us (2%)
    pallas_call x1, Pallas kernels, local(): pl.pallas_call(kernel, out_shape=jax.ShapeDtypeStruct((5, 4096), F32), in...  81.5 us

profile of v6, /device:TPU:0, one launch (start us, length us, event | category | flops | bytes accessed | tf_op | source)
XLA Modules:
  0.0 83.1 jit_solution(16019698695044456823)
XLA Ops:
  0.0 81.5 %shard_map.28 = f32[5,4096]{1,0:T(8,128)} custom-call(f32[2,256,4096]{2,1,0:T(8,128)} %g_hbm.1, bf16[2,256,640]{2,1,0:T(8,128)(2,1)} %w_hbm.1), custom_call_target="tpu_custom_call" | custom-call | flops 6499999744 | bytes 9200000 | tf_op jit(solution)/shard_map/pallas_call | solution.py:449
  81.6 1.6 %copy.4 = f32[5,4096]{1,0:T(8,128)} copy(f32[5,4096]{1,0:T(8,128)} %shard_map.28) | data formatting | bytes 163840

commit v7 on v6

--- a/solution.py
+++ b/solution.py
@@ -236,6 +236,8 @@
     pass_op(own + 1, s_aag.at[1], r_aag.at[1], z_down)
     pass_op(own + 1, s_aag.at[2], r_aag.at[2], z_up)
     pass_op(own, s_aag.at[3], r_aag.at[3], z_down)
+    for n in range(2):
+        pass_op(own + n, s_afw.at[n], r_afw.at[n], sibling)
     arrived(near.at[1, 3], r_one.at[7])
     whole_sum(3)
     second_axis(3)
@@ -290,8 +292,6 @@
     pass_op(below, s_aag.at[4], r_aag.at[4], z_up)
     arrived(a_op.at[above + 1], r_aag.at[1])
     pass_op(above + 1, s_aag.at[5], r_aag.at[5], z_down)
-    for n in range(2):
-        pass_op(own + n, s_afw.at[n], r_afw.at[n], sibling)
 
     pass_on(bg, s_b, r_b)
     spread(bl, s_l, r_l)

time: 83.6 us -> 83.6 us (level)
  no operation moved by 1% of the time
where the time goes in v7:
time: 83.6 us; the launch traced here: 83.1 us
  Pallas kernels  81.5 us (97%)
  local copies, waits for them, and re-layouts  1.57 us (2%)
    pallas_call x1, Pallas kernels, local(): pl.pallas_call(kernel, out_shape=jax.ShapeDtypeStruct((5, 4096), F32), in...  81.5 us

profile of v7, /device:TPU:0, one launch (start us, length us, event | category | flops | bytes accessed | tf_op | source)
XLA Modules:
  0.0 83.1 jit_solution(11568764949882702817)
XLA Ops:
  0.0 81.5 %shard_map.28 = f32[5,4096]{1,0:T(8,128)} custom-call(f32[2,256,4096]{2,1,0:T(8,128)} %g_hbm.1, bf16[2,256,640]{2,1,0:T(8,128)(2,1)} %w_hbm.1), custom_call_target="tpu_custom_call" | custom-call | flops 6499999744 | bytes 9200000 | tf_op jit(solution)/shard_map/pallas_call | solution.py:449
  81.6 1.6 %copy.4 = f32[5,4096]{1,0:T(8,128)} copy(f32[5,4096]{1,0:T(8,128)} %shard_map.28) | data formatting | bytes 163840
